TPU v7x, 32 devices: a whole 2x2x4 slice. The times are simulated.
32 devices in a mesh: space: 4 (over z), section: 4 (over y, x), rep: 2 (over core).
Axes of the slice: x: 2, y: 2, z: 4, core: 2. Of those that a mesh axis runs over, the one named last changes fastest.
Arguments:
- feats: bfloat16 [4, 16, 40, 256], P('rep', 'space'), may hold values from -6 to 6
- labels: int32 [4, 16, 40], P('rep', 'space'), may hold values from 0 to 2
- class_weight: int32 [3], replicated, may hold values from 1 to 9
- depth_kernel: bfloat16 [4, 3, 9, 256], P('section'), may hold values from -2 to 2
- point_weight: bfloat16 [4, 4, 256, 256], P('section'), may hold values from -0.375 to 0.375
- proj_weight: bfloat16 [4, 1024, 256], P('section'), may hold values from -0.1875 to 0.1875
- head_weight: bfloat16 [4, 256, 3], P('section'), may hold values from -0.375 to 0.375
Outputs:
- kernel_grad: float32 [4, 3, 9, 256], P('section')
- point_grad: float32 [4, 4, 256, 256], P('section')
- proj_grad: float32 [4, 1024, 256], P('section')
- head_grad: float32 [4, 256, 3], P('section')
All inputs are finite; a program needn't handle non-finite values.
Results may differ from a plain program's by a relative error of at most 0.013.
The roundings to bfloat16 on the way count: a program that leaves them out, or rounds other values in their place, can miss the bound.
Values may be sent and summed in bfloat16 or wider, within the bound.
A program may use at most 128 MiB of HBM per device.

v0:
```python
import jax
import jax.numpy as jnp
from jax import lax
from jax.sharding import PartitionSpec as P

spacings = (12, 24, 36)
loss_scale = 256.0


def passed_along(block, axis, distance):
    devices = range(lax.axis_size(axis))
    route = [(i - distance, i) for i in devices if i - distance in devices]
    return lax.ppermute(block, axis, route)


def moved(source, offset, axis_dim):
    length = source.shape[axis_dim]
    widths = [(0, 0)] * source.ndim
    widths[axis_dim] = (max(-offset, 0), max(offset, 0))
    padded = jnp.pad(source, widths)
    begin_at = max(offset, 0)
    return lax.slice_in_dim(padded, begin_at, begin_at + length, axis=axis_dim)


def make_view(shift_rows, device_count):

    def piece_from(source, devices_ahead):
        if devices_ahead >= device_count or -devices_ahead >= device_count:
            return jnp.zeros_like(source)
        return shift_rows(source, -devices_ahead)

    def view(source, offset):
        if offset == 0:
            return source
        tile_rows = source.shape[0]
        whole_part = offset // tile_rows
        return piece_from(source, whole_part)

    return view


def forward_taps(row_views, tap_weights, col_step):
    running = jnp.zeros(row_views[0].shape, jnp.float32)
    for row_tap in (-1, 0, 1):
        for col_tap in (-1, 0, 1):
            running = running + tap_weights[3 * (row_tap + 1) + col_tap + 1] * moved(
                row_views[row_tap], col_tap * col_step, 1
            )
    return running


def backward_taps(row_views, base_map, tap_weights, col_step):
    base_wide = base_map.astype(jnp.float32)
    running = jnp.zeros(base_map.shape, jnp.float32)
    kernel_rows = []
    for row_tap in (-1, 0, 1):
        for col_tap in (-1, 0, 1):
            shifted = moved(row_views[row_tap], -col_tap * col_step, 1)
            running = running + tap_weights[3 * (row_tap + 1) + col_tap + 1] * shifted
            partial_sum = jnp.sum(shifted * base_wide, axis=0)
            kernel_rows.append(jnp.sum(partial_sum, axis=0))
    return (running, jnp.stack(kernel_rows))


def matmul(first_op, second_op):
    return jnp.dot(first_op, second_op, preferred_element_type=jnp.float32)


def matmul_trans(first_op, second_op):
    return lax.dot_general(
        first_op, second_op, (((1,), (1,)), ((), ())), preferred_element_type=jnp.float32
    )


def outer(first_op, second_op):
    return lax.dot_general(
        first_op, second_op, (((0,), (0,)), ((), ())), preferred_element_type=jnp.float32
    )


def store(buffer, batch_slot, is_valid, new_value):
    old_value = lax.dynamic_index_in_dim(buffer, batch_slot, 0, keepdims=False)
    return lax.dynamic_update_index_in_dim(
        buffer, jnp.where(is_valid, new_value, old_value), batch_slot, 0
    )


def fetch(buffer, batch_slot):
    return lax.dynamic_index_in_dim(buffer, batch_slot, 0, keepdims=False)


def forward_block(current, weights, label_tile, tools, factor, weight_table):
    taps_all, flat_taps, point_mats, proj_mat, head_mat = weights
    view_fn, to_maps, from_maps = (tools[0], tools[1], tools[2])
    tile_rows, width_cols, channels = current.shape
    pixels = tile_rows * width_cols
    branch_list = []
    for branch, spacing in enumerate(spacings):
        row_views = {
            row_tap: view_fn(current, row_tap * spacing).astype(jnp.float32)
            for row_tap in (-1, 0, 1)
        }
        branch_list.append(forward_taps(row_views, taps_all[branch], spacing).astype(jnp.bfloat16))
    branch_out = jnp.stack(branch_list).reshape(3, pixels, channels)
    extra = ()
    flat_in = current.reshape(pixels, channels)
    pre_acts = [matmul(branch_out[branch], point_mats[branch]) for branch in range(3)]
    pre_acts.append(matmul(flat_in, point_mats[3]))
    joined = jnp.concatenate(
        [jnp.maximum(pre_act, 0.0).astype(jnp.bfloat16) for pre_act in pre_acts], axis=1
    )
    mixed_pre = matmul(joined, proj_mat)
    result = (flat_in.astype(jnp.float32) + jnp.maximum(mixed_pre, 0.0)).astype(jnp.bfloat16)
    logits = matmul(result, head_mat)
    class_ids = jnp.arange(3, dtype=jnp.int32)
    label_flat = label_tile.reshape(pixels, 1)
    onehot = (label_flat == class_ids[None, :]).astype(jnp.float32)
    pixel_weight = jnp.sum(onehot * weight_table[None, :], axis=1)
    chances = jax.nn.softmax(logits, axis=1)
    head_delta = ((factor * pixel_weight)[:, None] * (chances - onehot)).astype(jnp.bfloat16)
    head_term = outer(result, head_delta)
    from_head = matmul_trans(head_delta, head_mat)
    record = (current, branch_out, joined, mixed_pre, from_head) + extra
    return (result.reshape(tile_rows, width_cols, channels), head_term, record)


def backward_block(record, incoming, weights, tools):
    taps_all, flat_taps, point_mats, proj_mat, head_mat = weights
    view_fn, grads_to, grads_from = (tools[0], tools[3], tools[4])
    current, branch_out, joined, mixed_pre, from_head = (
        record[0],
        record[1],
        record[2],
        record[3],
        record[4],
    )
    tile_rows, width_cols, channels = current.shape
    pixels = tile_rows * width_cols
    total_grad = from_head + incoming
    gate_mixed = jnp.where(mixed_pre > 0, total_grad, 0.0).astype(jnp.bfloat16)
    proj_term = outer(joined, gate_mixed)
    back_joined = matmul_trans(gate_mixed, proj_mat)
    gate_joined = jnp.where(joined > 0, back_joined, 0.0).astype(jnp.bfloat16)
    flat_in = current.reshape(pixels, channels)
    point_terms = []
    branch_grads = []
    for branch in range(3):
        part_grad = gate_joined[:, branch * channels : (branch + 1) * channels]
        point_terms.append(outer(branch_out[branch], part_grad))
        branch_grads.append(matmul_trans(part_grad, point_mats[branch]).astype(jnp.bfloat16))
    part_grad = gate_joined[:, 3 * channels :]
    point_terms.append(outer(flat_in, part_grad))
    plain_back = matmul_trans(part_grad, point_mats[3])
    grads_stack = jnp.stack(branch_grads).reshape(3, tile_rows, width_cols, channels)
    spread = jnp.zeros((tile_rows, width_cols, channels), jnp.float32)
    kernel_terms = []
    for branch, spacing in enumerate(spacings):
        row_views = {
            row_tap: view_fn(grads_stack[branch], -row_tap * spacing).astype(jnp.float32)
            for row_tap in (-1, 0, 1)
        }
        back_map, tap_grad = backward_taps(row_views, current, taps_all[branch], spacing)
        spread = spread + back_map
        kernel_terms.append(tap_grad)
    kernel_term = jnp.stack(kernel_terms)
    input_grad = (total_grad + plain_back + spread.reshape(pixels, channels)).astype(jnp.bfloat16)
    return (
        input_grad.reshape(tile_rows, width_cols, channels),
        (kernel_term, jnp.stack(point_terms), proj_term),
    )


def per_device(feats, labels, class_weight, depth_kernel, point_weight, proj_weight, head_weight):
    micro_count, tile_rows, width_cols, channels = feats.shape
    space_count = lax.axis_size("space")
    section_count = lax.axis_size("section")
    section_place = lax.axis_index("section")
    factor = loss_scale / (
        micro_count * lax.axis_size("rep") * tile_rows * space_count * width_cols
    )
    weight_table = class_weight.astype(jnp.float32)
    share = channels // space_count
    channel_start = lax.axis_index("space") * share
    taps_all = depth_kernel[0].astype(jnp.float32)
    flat_taps = jnp.tile(
        lax.dynamic_slice_in_dim(taps_all, channel_start, share, 2), (1, 1, width_cols)
    )
    weights = (taps_all, flat_taps, point_weight[0], proj_weight[0], head_weight[0])

    def shift_space(source, devices_by):
        return passed_along(source, "space", devices_by)

    tools = (make_view(shift_space, space_count), None, None, None, None, share, channel_start)
    tick_total = micro_count + section_count - 1
    pixels = tile_rows * width_cols
    saved = None
    head_grad = jnp.zeros((channels, 3), jnp.float32)
    arriving = jnp.zeros((tile_rows, width_cols, channels), jnp.bfloat16)
    for moment in range(tick_total):
        batch_raw = moment - section_place
        is_valid = (batch_raw >= 0) & (batch_raw < micro_count)
        batch_slot = jnp.clip(batch_raw, 0, micro_count - 1)
        current = jnp.where(section_place == 0, feats[min(moment, micro_count - 1)], arriving)
        result, head_term, record = forward_block(
            current, weights, fetch(labels, batch_slot), tools, factor, weight_table
        )
        head_grad = head_grad + jnp.where(is_valid, head_term, 0.0)
        if saved is None:
            saved = tuple((jnp.zeros((micro_count,) + item.shape, item.dtype) for item in record))
        saved = tuple(
            (store(buffer, batch_slot, is_valid, item) for buffer, item in zip(saved, record))
        )
        if moment < tick_total - 1:
            arriving = passed_along(result, "section", 1)
    kernel_grad = jnp.zeros((3, 9, channels), jnp.float32)
    point_grad = jnp.zeros((4, channels, channels), jnp.float32)
    proj_grad = jnp.zeros((4 * channels, channels), jnp.float32)
    arriving_grad = jnp.zeros((tile_rows, width_cols, channels), jnp.bfloat16)
    for moment in range(tick_total):
        batch_raw = moment - (section_count - 1 - section_place)
        is_valid = (batch_raw >= 0) & (batch_raw < micro_count)
        batch_slot = jnp.clip(batch_raw, 0, micro_count - 1)
        record = tuple((fetch(buffer, batch_slot) for buffer in saved))
        incoming = arriving_grad.reshape(pixels, channels).astype(jnp.float32)
        input_grad, terms = backward_block(record, incoming, weights, tools)
        kernel_grad = kernel_grad + jnp.where(is_valid, terms[0], 0.0)
        point_grad = point_grad + jnp.where(is_valid, terms[1], 0.0)
        proj_grad = proj_grad + jnp.where(is_valid, terms[2], 0.0)
        if moment < tick_total - 1:
            arriving_grad = passed_along(input_grad, "section", -1)
    local_grads = (kernel_grad[None], point_grad[None], proj_grad[None], head_grad[None])
    summed = lax.psum(
        (local_grads[0], local_grads[1], local_grads[2], local_grads[3]), ("space", "rep")
    )
    return (summed[0], summed[1], summed[2], summed[3])


def solution(mesh):
    placed = (
        P("rep", "space", None, None),
        P("rep", "space", None),
        P(),
        P("section", None, None, None),
        P("section", None, None, None),
        P("section", None, None),
        P("section", None, None),
    )
    return jax.shard_map(
        per_device,
        mesh=mesh,
        in_specs=placed,
        out_specs=(
            P("section", None, None, None),
            P("section", None, None, None),
            P("section", None, None),
            P("section", None, None),
        ),
        check_vma=False,
    )
```

profile of v0, /device:TPU:0, one launch (start us, length us, event | category | flops | bytes accessed | tf_op | source)
XLA Modules:
  0.0 263.1 jit_solution(5001375919120492049)
XLA Ops:
  7.2 1.0 bitcast_convert_fusion.1
  8.2 1.3 collective-permute-start.1
  9.6 7.0 %collective-permute-start = (bf16[4,40,256]{2,1,0:T(8,128)(2,1)S(1)}, bf16[4,40,256]{2,1,0:T(8,128)(2,1)S(1)}, u32[]{:S(2)}, u32[]{:S(2)}) collective-permute-start(bf16[4,40,256]{2,1,0:T(8,128)(2,1)S(1)} %bitcast.832), channel_id=1, source_target_pairs={{0,24},{1,25},{2,26},{3,27},{4,28},{5,29},{6,30},{7,31}} | collective-permute-start | bytes 245768 | tf_op jit(solution)/shard_map/ppermute | solution.py:13
  22.3 4.2 %collective-permute-start.2 = (bf16[4,40,256]{2,1,0:T(8,128)(2,1)S(1)}, bf16[4,40,256]{2,1,0:T(8,128)(2,1)S(1)}, u32[]{:S(2)}, u32[]{:S(2)}) collective-permute-start(bf16[4,40,256]{2,1,0:T(8,128)(2,1)S(1)} %bitcast.1153), channel_id=1, source_target_pairs={{0,2},{2,4},{4,6},{1,3},{3,5},{5,7},{8,10},{10,12},{12,14},{9,11},... | collective-permute-start | bytes 245768 | tf_op jit(solution)/shard_map/ppermute | solution.py:13
  27.4 1.2 collective-permute-done.2
  28.8 1.3 collective-permute-start.4
  30.1 6.3 %collective-permute-start.3 = (bf16[4,40,256]{2,1,0:T(8,128)(2,1)S(1)}, bf16[4,40,256]{2,1,0:T(8,128)(2,1)S(1)}, u32[]{:S(2)}, u32[]{:S(2)}) collective-permute-start(bf16[4,40,256]{2,1,0:T(8,128)(2,1)S(1)} %get-tuple-element.181), channel_id=1, source_target_pairs={{0,24},{1,25},{2,26},{3,27},{4,28},{5,29},{6,30},{7,31}} | collective-permute-start | bytes 245768 | tf_op jit(solution)/shard_map/ppermute | solution.py:13
  37.1 1.4 collective-permute-done.3
  39.3 4.3 %collective-permute-start.5 = (bf16[4,40,256]{2,1,0:T(8,128)(2,1)S(1)}, bf16[4,40,256]{2,1,0:T(8,128)(2,1)S(1)}, u32[]{:S(2)}, u32[]{:S(2)}) collective-permute-start(bf16[4,40,256]{2,1,0:T(8,128)(2,1)S(1)} %bitcast.1154), channel_id=1, source_target_pairs={{0,2},{2,4},{4,6},{1,3},{3,5},{5,7},{8,10},{10,12},{12,14},{9,11},... | collective-permute-start | bytes 245768 | tf_op jit(solution)/shard_map/ppermute | solution.py:13
  45.8 1.3 collective-permute-start.7
  47.1 6.3 %collective-permute-start.6 = (bf16[4,40,256]{2,1,0:T(8,128)(2,1)S(1)}, bf16[4,40,256]{2,1,0:T(8,128)(2,1)S(1)}, u32[]{:S(2)}, u32[]{:S(2)}) collective-permute-start(bf16[4,40,256]{2,1,0:T(8,128)(2,1)S(1)} %get-tuple-element.179), channel_id=1, source_target_pairs={{0,24},{1,25},{2,26},{3,27},{4,28},{5,29},{6,30},{7,31}} | collective-permute-start | bytes 245768 | tf_op jit(solution)/shard_map/ppermute | solution.py:13
  54.0 1.4 collective-permute-done.6
  56.2 4.3 %collective-permute-start.8 = (bf16[4,40,256]{2,1,0:T(8,128)(2,1)S(1)}, bf16[4,40,256]{2,1,0:T(8,128)(2,1)S(1)}, u32[]{:S(2)}, u32[]{:S(2)}) collective-permute-start(bf16[4,40,256]{2,1,0:T(8,128)(2,1)S(1)} %bitcast.1155), channel_id=1, source_target_pairs={{0,2},{2,4},{4,6},{1,3},{3,5},{5,7},{8,10},{10,12},{12,14},{9,11},... | collective-permute-start | bytes 245768 | tf_op jit(solution)/shard_map/ppermute | solution.py:13
  62.8 1.3 collective-permute-start.10
  64.1 6.3 %collective-permute-start.9 = (bf16[4,40,256]{2,1,0:T(8,128)(2,1)S(1)}, bf16[4,40,256]{2,1,0:T(8,128)(2,1)S(1)}, u32[]{:S(2)}, u32[]{:S(2)}) collective-permute-start(bf16[4,40,256]{2,1,0:T(8,128)(2,1)S(1)} %get-tuple-element.177), channel_id=1, source_target_pairs={{0,24},{1,25},{2,26},{3,27},{4,28},{5,29},{6,30},{7,31}} | collective-permute-start | bytes 245768 | tf_op jit(solution)/shard_map/ppermute | solution.py:13
  71.0 1.4 collective-permute-done.9
  73.2 5.2 %collective-permute-start.11 = (bf16[4,40,256]{2,1,0:T(8,128)(2,1)S(1)}, bf16[4,40,256]{2,1,0:T(8,128)(2,1)S(1)}, u32[]{:S(2)}, u32[]{:S(2)}) collective-permute-start(bf16[4,40,256]{2,1,0:T(8,128)(2,1)S(1)} %bitcast.1156), channel_id=1, source_target_pairs={{0,2},{2,4},{4,6},{1,3},{3,5},{5,7},{8,10},{10,12},{12,14},{9,11},... | collective-permute-start | bytes 245768 | tf_op jit(solution)/shard_map/ppermute | solution.py:13
  79.1 1.4 collective-permute-done.11
  80.8 1.3 collective-permute-start.13
  82.1 6.3 %collective-permute-start.12 = (bf16[4,40,256]{2,1,0:T(8,128)(2,1)S(1)}, bf16[4,40,256]{2,1,0:T(8,128)(2,1)S(1)}, u32[]{:S(2)}, u32[]{:S(2)}) collective-permute-start(bf16[4,40,256]{2,1,0:T(8,128)(2,1)S(1)} %get-tuple-element.175), channel_id=1, source_target_pairs={{0,24},{1,25},{2,26},{3,27},{4,28},{5,29},{6,30},{7,31}} | collective-permute-start | bytes 245768 | tf_op jit(solution)/shard_map/ppermute | solution.py:13
  89.1 1.6 collective-permute-done.12
  92.4 6.2 %collective-permute-start.15 = (bf16[4,40,256]{2,1,0:T(8,128)(2,1)S(1)}, bf16[4,40,256]{2,1,0:T(8,128)(2,1)S(1)}, u32[]{:S(2)}, u32[]{:S(2)}) collective-permute-start(bf16[4,40,256]{2,1,0:T(8,128)(2,1)S(1)} %bitcast.877), channel_id=1, source_target_pairs={{0,24},{1,25},{2,26},{3,27},{4,28},{5,29},{6,30},{7,31}} | collective-permute-start | bytes 245768 | tf_op jit(solution)/shard_map/ppermute | solution.py:13
  98.6 1.3 collective-permute-start.14
  100.4 0.9 convolution_bitcast_fusion.19
  101.3 0.9 convolution_bitcast_fusion.18
  102.2 0.9 convolution_bitcast_fusion.17
  103.2 1.3 convolution_select_fusion.4
  104.5 0.7 fusion.53
  105.2 1.5 collective-permute-done.14
  107.9 0.8 fusion.374
  109.4 0.8 fusion.41
  110.2 2.6 stack.604
  112.8 1.3 stack.605
  114.1 1.3 collective-permute-start.16
  115.4 1.1 convolution_bitcast_fusion.16
  116.5 5.2 %collective-permute-done.16 = bf16[4,40,256]{2,1,0:T(8,128)(2,1)S(1)} collective-permute-done((bf16[4,40,256]{2,1,0:T(8,128)(2,1)}, bf16[4,40,256]{2,1,0:T(8,128)(2,1)S(1)}, u32[]{:S(2)}, u32[]{:S(2)}) %collective-permute-start.16) | collective-permute-done | bytes 81952 | tf_op jit(solution)/shard_map/ppermute | solution.py:13
  122.3 5.0 %collective-permute-start.18 = (bf16[4,40,256]{2,1,0:T(8,128)(2,1)S(1)}, bf16[4,40,256]{2,1,0:T(8,128)(2,1)S(1)}, u32[]{:S(2)}, u32[]{:S(2)}) collective-permute-start(bf16[4,40,256]{2,1,0:T(8,128)(2,1)S(1)} %bitcast.871), channel_id=1, source_target_pairs={{0,24},{1,25},{2,26},{3,27},{4,28},{5,29},{6,30},{7,31}} | collective-permute-start | bytes 245768 | tf_op jit(solution)/shard_map/ppermute | solution.py:13
  127.4 1.3 collective-permute-start.17
  130.2 5.3 %collective-permute-done.17 = bf16[4,40,256]{2,1,0:T(8,128)(2,1)S(1)} collective-permute-done((bf16[4,40,256]{2,1,0:T(8,128)(2,1)S(1)}, bf16[4,40,256]{2,1,0:T(8,128)(2,1)S(1)}, u32[]{:S(2)}, u32[]{:S(2)}) %collective-permute-start.17) | collective-permute-done | bytes 81952 | tf_op jit(solution)/shard_map/ppermute | solution.py:13
  136.9 1.5 collective-permute-start.19
  138.4 0.8 fusion.391
  139.8 4.6 %collective-permute-done.19 = bf16[4,40,256]{2,1,0:T(8,128)(2,1)S(1)} collective-permute-done((bf16[4,40,256]{2,1,0:T(8,128)(2,1)S(1)}, bf16[4,40,256]{2,1,0:T(8,128)(2,1)S(1)}, u32[]{:S(2)}, u32[]{:S(2)}) %collective-permute-start.19) | collective-permute-done | bytes 81952 | tf_op jit(solution)/shard_map/ppermute | solution.py:13
  145.1 1.5 collective-permute-start.21
  146.6 1.3 collective-permute-start.20
  149.2 5.5 %collective-permute-done.20 = bf16[4,40,256]{2,1,0:T(8,128)(2,1)S(1)} collective-permute-done((bf16[4,40,256]{2,1,0:T(8,128)(2,1)S(1)}, bf16[4,40,256]{2,1,0:T(8,128)(2,1)S(1)}, u32[]{:S(2)}, u32[]{:S(2)}) %collective-permute-start.20) | collective-permute-done | bytes 81952 | tf_op jit(solution)/shard_map/ppermute | solution.py:13
  156.9 1.3 collective-permute-start.22
  158.4 6.5 %collective-permute-done.22 = bf16[4,40,256]{2,1,0:T(8,128)(2,1)S(1)} collective-permute-done((bf16[4,40,256]{2,1,0:T(8,128)(2,1)S(1)}, bf16[4,40,256]{2,1,0:T(8,128)(2,1)S(1)}, u32[]{:S(2)}, u32[]{:S(2)}) %collective-permute-start.22) | collective-permute-done | bytes 81952 | tf_op jit(solution)/shard_map/ppermute | solution.py:13
  165.6 1.3 collective-permute-start.24
  166.9 1.3 collective-permute-start.23
  169.7 5.3 %collective-permute-done.23 = bf16[4,40,256]{2,1,0:T(8,128)(2,1)S(1)} collective-permute-done((bf16[4,40,256]{2,1,0:T(8,128)(2,1)S(1)}, bf16[4,40,256]{2,1,0:T(8,128)(2,1)S(1)}, u32[]{:S(2)}, u32[]{:S(2)}) %collective-permute-start.23) | collective-permute-done | bytes 81952 | tf_op jit(solution)/shard_map/ppermute | solution.py:13
  175.6 1.3 collective-permute-start.25
  176.9 0.8 fusion.425
  178.4 4.6 %collective-permute-done.25 = bf16[4,40,256]{2,1,0:T(8,128)(2,1)S(1)} collective-permute-done((bf16[4,40,256]{2,1,0:T(8,128)(2,1)S(1)}, bf16[4,40,256]{2,1,0:T(8,128)(2,1)S(1)}, u32[]{:S(2)}, u32[]{:S(2)}) %collective-permute-start.25) | collective-permute-done | bytes 81952 | tf_op jit(solution)/shard_map/ppermute | solution.py:13
  184.5 0.8 fusion.405
  185.8 1.3 fusion.1
  187.1 1.3 fusion.60
  188.5 0.9 copy-done.8
  191.8 1.7 collective-permute-start.27
  193.5 1.3 collective-permute-start.26
  200.9 2.2 collective-permute-done.26
  206.3 27.1 %all-reduce.104 = (f32[1,3,9,256]{3,0,2,1:T(1,128)}, f32[1,256,3]{1,2,0:T(4,128)S(1)}) all-reduce(f32[1,3,9,256]{3,0,2,1:T(1,128)S(1)} %fusion.561, f32[1,256,3]{1,2,0:T(4,128)S(1)} %copy-done.98), channel_id=1, replica_groups=mesh['space'=4,'section'=4,'rep'=2] {'space','rep'}, use_global_device_ids=true, to_apply=%region_115.116 | all-reduce | flops 7680 | bytes 61440 | tf_op jit(solution)/shard_map/psum | solution.py:232
  234.0 18.9 %all-reduce.108.cloned.1.call-done = (f32[1,4,256,256]{3,2,1,0:T(8,128)}, f32[1,1024,256]{2,1,0:T(8,128)}) async-done(((f32[1,4,256,256]{3,2,1,0:T(8,128)}, f32[1,1024,256]{2,1,0:T(8,128)}), (f32[1,4,256,256]{3,2,1,0:T(8,128)}, f32[1,1024,256]{2,1,0:T(8,128)})) %all-reduce.108.cloned.1.call-update) | async-done | bytes 2097168 | tf_op jit(solution)/shard_map/psum | solution.py:232
  252.9 2.4 copy.44
  255.3 1.0 copy.45
  (491 shorter events, 45.0 us)
Async XLA Ops:
  7.2 14.3 %copy-start = (bf16[1,1024,256]{2,1,0:T(8,128)(2,1)S(1)}, bf16[1,1024,256]{2,1,0:T(8,128)(2,1)}, u32[]{:S(2)}) copy-start(bf16[1,1024,256]{2,1,0:T(8,128)(2,1)} %param.12) | copy-start | bytes 1572868
  7.2 13.1 %copy-start.1 = (bf16[1,4,256,256]{3,2,1,0:T(8,128)(2,1)S(1)}, bf16[1,4,256,256]{3,2,1,0:T(8,128)(2,1)}, u32[]{:S(2)}) copy-start(bf16[1,4,256,256]{3,2,1,0:T(8,128)(2,1)} %param.11) | copy-start | bytes 1572868
  7.2 245.7 %all-reduce.108.cloned.1.call-start = ((), (), s32[]{:S(2)}) async-start(), calls=%async_computation | async-start | bytes 4194304 | tf_op jit(solution)/shard_map/psum | solution.py:232
  8.2 12.8 %collective-permute-start.1 = (bf16[4,40,256]{2,1,0:T(8,128)(2,1)S(1)}, bf16[4,40,256]{2,1,0:T(8,128)(2,1)S(1)}, u32[]{:S(2)}, u32[]{:S(2)}) collective-permute-start(bf16[4,40,256]{2,1,0:T(8,128)(2,1)S(1)} %bitcast.831), channel_id=1, source_target_pairs={{24,0},{25,1},{26,2},{27,3},{28,4},{29,5},{30,6},{31,7}} | collective-permute-start | bytes 245768 | tf_op jit(solution)/shard_map/ppermute | solution.py:13
  9.6 11.6 %collective-permute-start = (bf16[4,40,256]{2,1,0:T(8,128)(2,1)S(1)}, bf16[4,40,256]{2,1,0:T(8,128)(2,1)S(1)}, u32[]{:S(2)}, u32[]{:S(2)}) collective-permute-start(bf16[4,40,256]{2,1,0:T(8,128)(2,1)S(1)} %bitcast.832), channel_id=1, source_target_pairs={{0,24},{1,25},{2,26},{3,27},{4,28},{5,29},{6,30},{7,31}} | collective-permute-start | bytes 245768 | tf_op jit(solution)/shard_map/ppermute | solution.py:13
  17.3 63.2 %copy-start.35 = (f32[1,1,256]{2,0,1:T(1,128)}, f32[1,1,256]{2,0,1:T(1,128)S(1)}, u32[]{:S(2)}) copy-start(f32[1,1,256]{2,0,1:T(1,128)S(1)} %get-tuple-element.193) | copy-start | bytes 3076
  17.4 63.2 %copy-start.38 = (f32[1,1,256]{2,0,1:T(1,128)}, f32[1,1,256]{2,0,1:T(1,128)S(1)}, u32[]{:S(2)}) copy-start(f32[1,1,256]{2,0,1:T(1,128)S(1)} %get-tuple-element.194) | copy-start | bytes 3076
  17.4 63.2 %copy-start.41 = (f32[1,1,256]{2,0,1:T(1,128)}, f32[1,1,256]{2,0,1:T(1,128)S(1)}, u32[]{:S(2)}) copy-start(f32[1,1,256]{2,0,1:T(1,128)S(1)} %get-tuple-element.195) | copy-start | bytes 3076
  17.4 63.2 %copy-start.44 = (f32[1,1,256]{2,0,1:T(1,128)}, f32[1,1,256]{2,0,1:T(1,128)S(1)}, u32[]{:S(2)}) copy-start(f32[1,1,256]{2,0,1:T(1,128)S(1)} %get-tuple-element.196) | copy-start | bytes 3076
  17.4 63.2 %copy-start.47 = (f32[1,1,256]{2,0,1:T(1,128)}, f32[1,1,256]{2,0,1:T(1,128)S(1)}, u32[]{:S(2)}) copy-start(f32[1,1,256]{2,0,1:T(1,128)S(1)} %get-tuple-element.197) | copy-start | bytes 3076
  17.4 63.2 %copy-start.50 = (f32[1,1,256]{2,0,1:T(1,128)}, f32[1,1,256]{2,0,1:T(1,128)S(1)}, u32[]{:S(2)}) copy-start(f32[1,1,256]{2,0,1:T(1,128)S(1)} %get-tuple-element.198) | copy-start | bytes 3076
  17.4 63.2 %copy-start.53 = (f32[1,1,256]{2,0,1:T(1,128)}, f32[1,1,256]{2,0,1:T(1,128)S(1)}, u32[]{:S(2)}) copy-start(f32[1,1,256]{2,0,1:T(1,128)S(1)} %get-tuple-element.199) | copy-start | bytes 3076
  17.4 63.2 %copy-start.56 = (f32[1,1,256]{2,0,1:T(1,128)}, f32[1,1,256]{2,0,1:T(1,128)S(1)}, u32[]{:S(2)}) copy-start(f32[1,1,256]{2,0,1:T(1,128)S(1)} %get-tuple-element.200) | copy-start | bytes 3076
  17.4 63.2 %copy-start.59 = (f32[1,1,256]{2,0,1:T(1,128)}, f32[1,1,256]{2,0,1:T(1,128)S(1)}, u32[]{:S(2)}) copy-start(f32[1,1,256]{2,0,1:T(1,128)S(1)} %get-tuple-element.201) | copy-start | bytes 3076
  17.4 63.2 %copy-start.62 = (f32[1,1,256]{2,0,1:T(1,128)}, f32[1,1,256]{2,0,1:T(1,128)S(1)}, u32[]{:S(2)}) copy-start(f32[1,1,256]{2,0,1:T(1,128)S(1)} %get-tuple-element.202) | copy-start | bytes 3076
  17.4 63.2 %copy-start.65 = (f32[1,1,256]{2,0,1:T(1,128)}, f32[1,1,256]{2,0,1:T(1,128)S(1)}, u32[]{:S(2)}) copy-start(f32[1,1,256]{2,0,1:T(1,128)S(1)} %get-tuple-element.203) | copy-start | bytes 3076
  17.5 63.2 %copy-start.68 = (f32[1,1,256]{2,0,1:T(1,128)}, f32[1,1,256]{2,0,1:T(1,128)S(1)}, u32[]{:S(2)}) copy-start(f32[1,1,256]{2,0,1:T(1,128)S(1)} %get-tuple-element.204) | copy-start | bytes 3076
  17.5 63.2 %copy-start.71 = (f32[1,1,256]{2,0,1:T(1,128)}, f32[1,1,256]{2,0,1:T(1,128)S(1)}, u32[]{:S(2)}) copy-start(f32[1,1,256]{2,0,1:T(1,128)S(1)} %get-tuple-element.205) | copy-start | bytes 3076
  17.5 63.2 %copy-start.74 = (f32[1,1,256]{2,0,1:T(1,128)}, f32[1,1,256]{2,0,1:T(1,128)S(1)}, u32[]{:S(2)}) copy-start(f32[1,1,256]{2,0,1:T(1,128)S(1)} %get-tuple-element.206) | copy-start | bytes 3076
  17.5 63.2 %copy-start.77 = (f32[1,1,256]{2,0,1:T(1,128)}, f32[1,1,256]{2,0,1:T(1,128)S(1)}, u32[]{:S(2)}) copy-start(f32[1,1,256]{2,0,1:T(1,128)S(1)} %get-tuple-element.207) | copy-start | bytes 3076
  18.5 72.9 %copy-start.83 = (s32[160]{0:T(256)}, s32[160]{0:T(256)S(1)}, u32[]{:S(2)}) copy-start(s32[160]{0:T(256)S(1)} %eq.99) | copy-start | bytes 1924
  22.3 6.3 %collective-permute-start.2 = (bf16[4,40,256]{2,1,0:T(8,128)(2,1)S(1)}, bf16[4,40,256]{2,1,0:T(8,128)(2,1)S(1)}, u32[]{:S(2)}, u32[]{:S(2)}) collective-permute-start(bf16[4,40,256]{2,1,0:T(8,128)(2,1)S(1)} %bitcast.1153), channel_id=1, source_target_pairs={{0,2},{2,4},{4,6},{1,3},{3,5},{5,7},{8,10},{10,12},{12,14},{9,11},... | collective-permute-start | bytes 245768 | tf_op jit(solution)/shard_map/ppermute | solution.py:13
  28.8 8.2 %collective-permute-start.4 = (bf16[4,40,256]{2,1,0:T(8,128)(2,1)S(1)}, bf16[4,40,256]{2,1,0:T(8,128)(2,1)S(1)}, u32[]{:S(2)}, u32[]{:S(2)}) collective-permute-start(bf16[4,40,256]{2,1,0:T(8,128)(2,1)S(1)} %get-tuple-element.181), channel_id=1, source_target_pairs={{24,0},{25,1},{26,2},{27,3},{28,4},{29,5},{30,6},{31,7}} | collective-permute-start | bytes 245768 | tf_op jit(solution)/shard_map/ppermute | solution.py:13
  30.1 8.4 %collective-permute-start.3 = (bf16[4,40,256]{2,1,0:T(8,128)(2,1)S(1)}, bf16[4,40,256]{2,1,0:T(8,128)(2,1)S(1)}, u32[]{:S(2)}, u32[]{:S(2)}) collective-permute-start(bf16[4,40,256]{2,1,0:T(8,128)(2,1)S(1)} %get-tuple-element.181), channel_id=1, source_target_pairs={{0,24},{1,25},{2,26},{3,27},{4,28},{5,29},{6,30},{7,31}} | collective-permute-start | bytes 245768 | tf_op jit(solution)/shard_map/ppermute | solution.py:13
  39.3 6.3 %collective-permute-start.5 = (bf16[4,40,256]{2,1,0:T(8,128)(2,1)S(1)}, bf16[4,40,256]{2,1,0:T(8,128)(2,1)S(1)}, u32[]{:S(2)}, u32[]{:S(2)}) collective-permute-start(bf16[4,40,256]{2,1,0:T(8,128)(2,1)S(1)} %bitcast.1154), channel_id=1, source_target_pairs={{0,2},{2,4},{4,6},{1,3},{3,5},{5,7},{8,10},{10,12},{12,14},{9,11},... | collective-permute-start | bytes 245768 | tf_op jit(solution)/shard_map/ppermute | solution.py:13
  45.8 8.2 %collective-permute-start.7 = (bf16[4,40,256]{2,1,0:T(8,128)(2,1)S(1)}, bf16[4,40,256]{2,1,0:T(8,128)(2,1)S(1)}, u32[]{:S(2)}, u32[]{:S(2)}) collective-permute-start(bf16[4,40,256]{2,1,0:T(8,128)(2,1)S(1)} %get-tuple-element.179), channel_id=1, source_target_pairs={{24,0},{25,1},{26,2},{27,3},{28,4},{29,5},{30,6},{31,7}} | collective-permute-start | bytes 245768 | tf_op jit(solution)/shard_map/ppermute | solution.py:13
  47.1 8.4 %collective-permute-start.6 = (bf16[4,40,256]{2,1,0:T(8,128)(2,1)S(1)}, bf16[4,40,256]{2,1,0:T(8,128)(2,1)S(1)}, u32[]{:S(2)}, u32[]{:S(2)}) collective-permute-start(bf16[4,40,256]{2,1,0:T(8,128)(2,1)S(1)} %get-tuple-element.179), channel_id=1, source_target_pairs={{0,24},{1,25},{2,26},{3,27},{4,28},{5,29},{6,30},{7,31}} | collective-permute-start | bytes 245768 | tf_op jit(solution)/shard_map/ppermute | solution.py:13
  56.2 6.4 %collective-permute-start.8 = (bf16[4,40,256]{2,1,0:T(8,128)(2,1)S(1)}, bf16[4,40,256]{2,1,0:T(8,128)(2,1)S(1)}, u32[]{:S(2)}, u32[]{:S(2)}) collective-permute-start(bf16[4,40,256]{2,1,0:T(8,128)(2,1)S(1)} %bitcast.1155), channel_id=1, source_target_pairs={{0,2},{2,4},{4,6},{1,3},{3,5},{5,7},{8,10},{10,12},{12,14},{9,11},... | collective-permute-start | bytes 245768 | tf_op jit(solution)/shard_map/ppermute | solution.py:13
  62.8 8.2 %collective-permute-start.10 = (bf16[4,40,256]{2,1,0:T(8,128)(2,1)S(1)}, bf16[4,40,256]{2,1,0:T(8,128)(2,1)S(1)}, u32[]{:S(2)}, u32[]{:S(2)}) collective-permute-start(bf16[4,40,256]{2,1,0:T(8,128)(2,1)S(1)} %get-tuple-element.177), channel_id=1, source_target_pairs={{24,0},{25,1},{26,2},{27,3},{28,4},{29,5},{30,6},{31,7}} | collective-permute-start | bytes 245768 | tf_op jit(solution)/shard_map/ppermute | solution.py:13
  64.1 8.4 %collective-permute-start.9 = (bf16[4,40,256]{2,1,0:T(8,128)(2,1)S(1)}, bf16[4,40,256]{2,1,0:T(8,128)(2,1)S(1)}, u32[]{:S(2)}, u32[]{:S(2)}) collective-permute-start(bf16[4,40,256]{2,1,0:T(8,128)(2,1)S(1)} %get-tuple-element.177), channel_id=1, source_target_pairs={{0,24},{1,25},{2,26},{3,27},{4,28},{5,29},{6,30},{7,31}} | collective-permute-start | bytes 245768 | tf_op jit(solution)/shard_map/ppermute | solution.py:13
  73.2 7.3 %collective-permute-start.11 = (bf16[4,40,256]{2,1,0:T(8,128)(2,1)S(1)}, bf16[4,40,256]{2,1,0:T(8,128)(2,1)S(1)}, u32[]{:S(2)}, u32[]{:S(2)}) collective-permute-start(bf16[4,40,256]{2,1,0:T(8,128)(2,1)S(1)} %bitcast.1156), channel_id=1, source_target_pairs={{0,2},{2,4},{4,6},{1,3},{3,5},{5,7},{8,10},{10,12},{12,14},{9,11},... | collective-permute-start | bytes 245768 | tf_op jit(solution)/shard_map/ppermute | solution.py:13
  80.8 8.2 %collective-permute-start.13 = (bf16[4,40,256]{2,1,0:T(8,128)(2,1)S(1)}, bf16[4,40,256]{2,1,0:T(8,128)(2,1)S(1)}, u32[]{:S(2)}, u32[]{:S(2)}) collective-permute-start(bf16[4,40,256]{2,1,0:T(8,128)(2,1)S(1)} %get-tuple-element.175), channel_id=1, source_target_pairs={{24,0},{25,1},{26,2},{27,3},{28,4},{29,5},{30,6},{31,7}} | collective-permute-start | bytes 245768 | tf_op jit(solution)/shard_map/ppermute | solution.py:13
  82.1 8.5 %collective-permute-start.12 = (bf16[4,40,256]{2,1,0:T(8,128)(2,1)S(1)}, bf16[4,40,256]{2,1,0:T(8,128)(2,1)S(1)}, u32[]{:S(2)}, u32[]{:S(2)}) collective-permute-start(bf16[4,40,256]{2,1,0:T(8,128)(2,1)S(1)} %get-tuple-element.175), channel_id=1, source_target_pairs={{0,24},{1,25},{2,26},{3,27},{4,28},{5,29},{6,30},{7,31}} | collective-permute-start | bytes 245768 | tf_op jit(solution)/shard_map/ppermute | solution.py:13
  92.4 14.3 %collective-permute-start.15 = (bf16[4,40,256]{2,1,0:T(8,128)(2,1)S(1)}, bf16[4,40,256]{2,1,0:T(8,128)(2,1)S(1)}, u32[]{:S(2)}, u32[]{:S(2)}) collective-permute-start(bf16[4,40,256]{2,1,0:T(8,128)(2,1)S(1)} %bitcast.877), channel_id=1, source_target_pairs={{0,24},{1,25},{2,26},{3,27},{4,28},{5,29},{6,30},{7,31}} | collective-permute-start | bytes 245768 | tf_op jit(solution)/shard_map/ppermute | solution.py:13
  98.6 8.1 %collective-permute-start.14 = (bf16[4,40,256]{2,1,0:T(8,128)(2,1)S(1)}, bf16[4,40,256]{2,1,0:T(8,128)(2,1)S(1)}, u32[]{:S(2)}, u32[]{:S(2)}) collective-permute-start(bf16[4,40,256]{2,1,0:T(8,128)(2,1)S(1)} %bitcast.878), channel_id=1, source_target_pairs={{24,0},{25,1},{26,2},{27,3},{28,4},{29,5},{30,6},{31,7}} | collective-permute-start | bytes 245768 | tf_op jit(solution)/shard_map/ppermute | solution.py:13
  114.1 7.6 %collective-permute-start.16 = (bf16[4,40,256]{2,1,0:T(8,128)(2,1)}, bf16[4,40,256]{2,1,0:T(8,128)(2,1)S(1)}, u32[]{:S(2)}, u32[]{:S(2)}) collective-permute-start(bf16[4,40,256]{2,1,0:T(8,128)(2,1)} %bitcast.1158), channel_id=1, source_target_pairs={{2,0},{4,2},{6,4},{3,1},{5,3},{7,5},{10,8},{12,10},{14,12},{11,9},... | collective-permute-start | bytes 245768 | tf_op jit(solution)/shard_map/ppermute | solution.py:13
  122.1 7.5 %copy-start.2 = (f32[1024,256]{1,0:T(8,128)S(1)}, f32[1024,256]{1,0:T(8,128)}, u32[]{:S(2)}) copy-start(f32[1024,256]{1,0:T(8,128)} %convolution_select_fusion.4) | copy-start | bytes 3145732
  122.3 6.3 %copy-start.26 = (bf16[160,256]{1,0:T(8,128)(2,1)}, bf16[160,256]{1,0:T(8,128)(2,1)S(1)}, u32[]{:S(2)}) copy-start(bf16[160,256]{1,0:T(8,128)(2,1)S(1)} %convolution_convert_fusion.11) | copy-start | bytes 245764
  122.3 13.3 %collective-permute-start.18 = (bf16[4,40,256]{2,1,0:T(8,128)(2,1)S(1)}, bf16[4,40,256]{2,1,0:T(8,128)(2,1)S(1)}, u32[]{:S(2)}, u32[]{:S(2)}) collective-permute-start(bf16[4,40,256]{2,1,0:T(8,128)(2,1)S(1)} %bitcast.871), channel_id=1, source_target_pairs={{0,24},{1,25},{2,26},{3,27},{4,28},{5,29},{6,30},{7,31}} | collective-permute-start | bytes 245768 | tf_op jit(solution)/shard_map/ppermute | solution.py:13
  127.4 8.1 %collective-permute-start.17 = (bf16[4,40,256]{2,1,0:T(8,128)(2,1)S(1)}, bf16[4,40,256]{2,1,0:T(8,128)(2,1)S(1)}, u32[]{:S(2)}, u32[]{:S(2)}) collective-permute-start(bf16[4,40,256]{2,1,0:T(8,128)(2,1)S(1)} %bitcast.872), channel_id=1, source_target_pairs={{24,0},{25,1},{26,2},{27,3},{28,4},{29,5},{30,6},{31,7}} | collective-permute-start | bytes 245768 | tf_op jit(solution)/shard_map/ppermute | solution.py:13
  128.9 9.5 %copy-start.7 = (f32[160,256]{1,0:T(8,128)}, f32[160,256]{1,0:T(8,128)S(1)}, u32[]{:S(2)}) copy-start(f32[160,256]{1,0:T(8,128)S(1)} %fusion.48) | copy-start | bytes 491524
  129.1 9.3 %copy-start.9 = (f32[160,256]{1,0:T(8,128)}, f32[160,256]{1,0:T(8,128)S(1)}, u32[]{:S(2)}) copy-start(f32[160,256]{1,0:T(8,128)S(1)} %fusion.49) | copy-start | bytes 491524
  136.9 7.6 %collective-permute-start.19 = (bf16[4,40,256]{2,1,0:T(8,128)(2,1)S(1)}, bf16[4,40,256]{2,1,0:T(8,128)(2,1)S(1)}, u32[]{:S(2)}, u32[]{:S(2)}) collective-permute-start(bf16[4,40,256]{2,1,0:T(8,128)(2,1)S(1)} %bitcast.1151), channel_id=1, source_target_pairs={{2,0},{4,2},{6,4},{3,1},{5,3},{7,5},{10,8},{12,10},{14,12},{11,9},... | collective-permute-start | bytes 245768 | tf_op jit(solution)/shard_map/ppermute | solution.py:13
  145.1 2.9 %copy-start.24 = (bf16[160,256]{1,0:T(8,128)(2,1)}, bf16[160,256]{1,0:T(8,128)(2,1)S(1)}, u32[]{:S(2)}) copy-start(bf16[160,256]{1,0:T(8,128)(2,1)S(1)} %convolution_convert_fusion.8) | copy-start | bytes 245764
  145.1 10.3 %collective-permute-start.21 = (bf16[4,40,256]{2,1,0:T(8,128)(2,1)S(1)}, bf16[4,40,256]{2,1,0:T(8,128)(2,1)S(1)}, u32[]{:S(2)}, u32[]{:S(2)}) collective-permute-start(bf16[4,40,256]{2,1,0:T(8,128)(2,1)S(1)} %bitcast.868), channel_id=1, source_target_pairs={{0,24},{1,25},{2,26},{3,27},{4,28},{5,29},{6,30},{7,31}} | collective-permute-start | bytes 245768 | tf_op jit(solution)/shard_map/ppermute | solution.py:13
  146.6 8.1 %collective-permute-start.20 = (bf16[4,40,256]{2,1,0:T(8,128)(2,1)S(1)}, bf16[4,40,256]{2,1,0:T(8,128)(2,1)S(1)}, u32[]{:S(2)}, u32[]{:S(2)}) collective-permute-start(bf16[4,40,256]{2,1,0:T(8,128)(2,1)S(1)} %bitcast.869), channel_id=1, source_target_pairs={{24,0},{25,1},{26,2},{27,3},{28,4},{29,5},{30,6},{31,7}} | collective-permute-start | bytes 245768 | tf_op jit(solution)/shard_map/ppermute | solution.py:13
  156.9 8.1 %collective-permute-start.22 = (bf16[4,40,256]{2,1,0:T(8,128)(2,1)S(1)}, bf16[4,40,256]{2,1,0:T(8,128)(2,1)S(1)}, u32[]{:S(2)}, u32[]{:S(2)}) collective-permute-start(bf16[4,40,256]{2,1,0:T(8,128)(2,1)S(1)} %bitcast.1152), channel_id=1, source_target_pairs={{2,0},{4,2},{6,4},{3,1},{5,3},{7,5},{10,8},{12,10},{14,12},{11,9},... | collective-permute-start | bytes 245768 | tf_op jit(solution)/shard_map/ppermute | solution.py:13
  165.6 2.6 %copy-start.28 = (bf16[160,256]{1,0:T(8,128)(2,1)}, bf16[160,256]{1,0:T(8,128)(2,1)S(1)}, u32[]{:S(2)}) copy-start(bf16[160,256]{1,0:T(8,128)(2,1)S(1)} %convolution_convert_fusion.5) | copy-start | bytes 245764
  165.6 9.5 %collective-permute-start.24 = (bf16[4,40,256]{2,1,0:T(8,128)(2,1)S(1)}, bf16[4,40,256]{2,1,0:T(8,128)(2,1)S(1)}, u32[]{:S(2)}, u32[]{:S(2)}) collective-permute-start(bf16[4,40,256]{2,1,0:T(8,128)(2,1)S(1)} %bitcast.874), channel_id=1, source_target_pairs={{0,24},{1,25},{2,26},{3,27},{4,28},{5,29},{6,30},{7,31}} | collective-permute-start | bytes 245768 | tf_op jit(solution)/shard_map/ppermute | solution.py:13
  166.9 8.1 %collective-permute-start.23 = (bf16[4,40,256]{2,1,0:T(8,128)(2,1)S(1)}, bf16[4,40,256]{2,1,0:T(8,128)(2,1)S(1)}, u32[]{:S(2)}, u32[]{:S(2)}) collective-permute-start(bf16[4,40,256]{2,1,0:T(8,128)(2,1)S(1)} %bitcast.875), channel_id=1, source_target_pairs={{24,0},{25,1},{26,2},{27,3},{28,4},{29,5},{30,6},{31,7}} | collective-permute-start | bytes 245768 | tf_op jit(solution)/shard_map/ppermute | solution.py:13
  168.4 8.5 %copy-start.3 = (f32[160,256]{1,0:T(8,128)}, f32[160,256]{1,0:T(8,128)S(1)}, u32[]{:S(2)}) copy-start(f32[160,256]{1,0:T(8,128)S(1)} %fusion.44) | copy-start | bytes 491524
  168.6 8.3 %copy-start.5 = (f32[160,256]{1,0:T(8,128)}, f32[160,256]{1,0:T(8,128)S(1)}, u32[]{:S(2)}) copy-start(f32[160,256]{1,0:T(8,128)S(1)} %fusion.45) | copy-start | bytes 491524
  175.6 7.4 %collective-permute-start.25 = (bf16[4,40,256]{2,1,0:T(8,128)(2,1)S(1)}, bf16[4,40,256]{2,1,0:T(8,128)(2,1)S(1)}, u32[]{:S(2)}, u32[]{:S(2)}) collective-permute-start(bf16[4,40,256]{2,1,0:T(8,128)(2,1)S(1)} %bitcast.1150), channel_id=1, source_target_pairs={{2,0},{4,2},{6,4},{3,1},{5,3},{7,5},{10,8},{12,10},{14,12},{11,9},... | collective-permute-start | bytes 245768 | tf_op jit(solution)/shard_map/ppermute | solution.py:13
  191.5 3.3 %copy-start.31 = (bf16[4,40,256]{2,1,0:T(8,128)(2,1)S(1)}, bf16[4,40,256]{2,1,0:T(8,128)(2,1)}, u32[]{:S(2)}) copy-start(bf16[4,40,256]{2,1,0:T(8,128)(2,1)} %copy-done.30) | copy-start | bytes 245764
  191.5 3.3 %copy-start.33 = (bf16[4,40,256]{2,1,0:T(8,128)(2,1)S(1)}, bf16[4,40,256]{2,1,0:T(8,128)(2,1)}, u32[]{:S(2)}) copy-start(bf16[4,40,256]{2,1,0:T(8,128)(2,1)} %copy-done.32) | copy-start | bytes 245764
  191.8 3.0 %copy-start.12 = (f32[4,40,256]{2,1,0:T(8,128)S(1)}, f32[4,40,256]{2,1,0:T(8,128)}, u32[]{:S(2)}) copy-start(f32[4,40,256]{2,1,0:T(8,128)} %copy-done.11) | copy-start | bytes 491524
  191.8 3.0 %copy-start.16 = (bf16[1,4,40,256]{3,2,1,0:T(8,128)(2,1)S(1)}, bf16[1,4,40,256]{3,2,1,0:T(8,128)(2,1)}, u32[]{:S(2)}) copy-start(bf16[1,4,40,256]{3,2,1,0:T(8,128)(2,1)} %copy-done.15) | copy-start | bytes 245764
  191.8 11.3 %collective-permute-start.27 = (bf16[4,40,256]{2,1,0:T(8,128)(2,1)S(1)}, bf16[4,40,256]{2,1,0:T(8,128)(2,1)S(1)}, u32[]{:S(2)}, u32[]{:S(2)}) collective-permute-start(bf16[4,40,256]{2,1,0:T(8,128)(2,1)S(1)} %bitcast.904), channel_id=1, source_target_pairs={{0,24},{1,25},{2,26},{3,27},{4,28},{5,29},{6,30},{7,31}} | collective-permute-start | bytes 245768 | tf_op jit(solution)/shard_map/ppermute | solution.py:13
  193.5 9.6 %collective-permute-start.26 = (bf16[4,40,256]{2,1,0:T(8,128)(2,1)S(1)}, bf16[4,40,256]{2,1,0:T(8,128)(2,1)S(1)}, u32[]{:S(2)}, u32[]{:S(2)}) collective-permute-start(bf16[4,40,256]{2,1,0:T(8,128)(2,1)S(1)} %bitcast.905), channel_id=1, source_target_pairs={{24,0},{25,1},{26,2},{27,3},{28,4},{29,5},{30,6},{31,7}} | collective-permute-start | bytes 245768 | tf_op jit(solution)/shard_map/ppermute | solution.py:13
  195.7 1.6 copy-start.88
  195.8 1.6 copy-start.91
  195.8 3.7 %copy-start.102 = (f32[256]{0:T(256)S(1)}, f32[256]{0:T(256)}, u32[]{:S(2)}) copy-start(f32[256]{0:T(256)} %get-tuple-element.122) | copy-start | bytes 3076
  196.5 3.6 %copy-start.100 = (f32[256]{0:T(256)S(1)}, f32[256]{0:T(256)}, u32[]{:S(2)}) copy-start(f32[256]{0:T(256)} %get-tuple-element.120) | copy-start | bytes 3076
  252.9 2.4 copy-start.22
  (89 other events, 67.8 us)
Sparse Core Ops, SparseCore 0:
  188.6 64.2 all-reduce.107
where the time goes:
time: 264 us; the launch traced here: 263 us
  starting transfers between devices  84.4 us (32%)
  waiting for transfers between devices  69.5 us (26%)
  blocking collectives  27.1 us (10%)
  local copies, waits for them, and re-layouts  26.4 us (10%)
  matrix products  25.3 us (10%)
  between operations  16.6 us (6%)
  other arithmetic  13.7 us (5%)
    ppermute x28, starting transfers between devices, passed_along(): return lax.ppermute(block, axis, route)  84.4 us
    ppermute x28, waiting for transfers between devices, passed_along(): return lax.ppermute(block, axis, route)  50.6 us
    psum x1, blocking collectives, per_device(): lax.psum((local_grads[0], local_grads[1], local_grads[2], local_grads[3])...  27.1 us
    unnamed x251, local copies, waits for them, and re-layouts  21 us
    psum x1, waiting for transfers between devices, per_device(): lax.psum((local_grads[0], local_grads[1], local_grads[2], local_grads[3])...  18.9 us
    dot_general x30, matrix products, outer(): lax.dot_general(first_op, second_op, (((0,), (0,)), ((), ())), preferred_...  12.6 us
    dot_general x29, matrix products, matmul_trans(): lax.dot_general(first_op, second_op, (((1,), (1,)), ((), ())), preferred_...  7.32 us
    dot_general x30, matrix products, matmul(): return jnp.dot(first_op, second_op, preferred_element_type=jnp.float32)  5.46 us
  transfers between devices with their start and end apart: 29, of which 18 were waited for; matrix products, arithmetic and copies ran while one was open for 9% of the time, Pallas kernels for 0%

commit v1 on v0

--- a/solution.py
+++ b/solution.py
@@ -1,6 +1,10 @@
+import functools
+
 import jax
 import jax.numpy as jnp
 from jax import lax
+from jax.experimental import pallas as pl
+from jax.experimental.pallas import tpu as pltpu
 from jax.sharding import PartitionSpec as P
 
 spacings = (12, 24, 36)
@@ -170,7 +174,7 @@
     )
 
 
-def per_device(feats, labels, class_weight, depth_kernel, point_weight, proj_weight, head_weight):
+def general_program(feats, labels, class_weight, depth_kernel, point_weight, proj_weight, head_weight):
     micro_count, tile_rows, width_cols, channels = feats.shape
     space_count = lax.axis_size("space")
     section_count = lax.axis_size("section")
@@ -235,6 +239,391 @@
     return (summed[0], summed[1], summed[2], summed[3])
 
 
+GROUPS = 2
+SHARD = 272
+EXTRA = 2048
+HEAD_ROW = EXTRA + 32
+NT = (((1,), (1,)), ((), ()))
+TN = (((0,), (0,)), ((), ()))
+F32 = jnp.float32
+BF16 = jnp.bfloat16
+
+
+def rows_from(values, offset):
+    if offset == 0:
+        return values
+    blank = jnp.zeros((abs(offset), values.shape[1]), values.dtype)
+    if offset > 0:
+        return jnp.concatenate([values[offset:], blank], axis=0)
+    return jnp.concatenate([blank, values[:offset]], axis=0)
+
+
+def lagged_sum(first, second, offset):
+    length = first.shape[0]
+    if offset >= 0:
+        product = first[: length - offset] * second[offset:]
+    else:
+        product = first[-offset:] * second[:offset]
+    return jnp.sum(product, axis=0, keepdims=True)
+
+
+def dot(first, second, dims=(((1,), (0,)), ((), ()))):
+    return lax.dot_general(first, second, dims, preferred_element_type=F32)
+
+
+def block_kernel(
+    factor, spaces, sections,
+    feats, labels, class_weight, taps, point, proj, head,
+    out_point, out_proj, out_extra,
+    xbuf, gbuf, xout, gout, lab, us, vs, ms, hs, total, wide, pair_in, half, ring_in, full,
+    feat_send, feat_recv, lab_send, lab_recv, x_send, x_recv, g_send, g_recv,
+    p_send, p_recv, r_send, r_recv, a_send, a_recv, c_send, c_recv,
+):
+    space = lax.axis_index("space")
+    section = lax.axis_index("section")
+    rep = lax.axis_index("rep")
+    last = sections - 1
+    step = xbuf.shape[2] // 40
+    slot_rows = xbuf.shape[2]
+    pixels = 2 * slot_rows
+    after = {"section": lax.rem(section + 1, sections)}
+    before = {"section": lax.rem(section + sections - 1, sections)}
+    twin = {"rep": 1 - rep}
+
+    def along(distance):
+        return {"space": lax.rem(space + distance, spaces)}
+
+    def remote(source, target, send, recv, device):
+        return pltpu.make_async_remote_copy(
+            src_ref=source, dst_ref=target, send_sem=send, recv_sem=recv,
+            device_id=device, device_id_type=pl.DeviceIdType.MESH,
+        )
+
+    barrier = pltpu.get_barrier_semaphore()
+    greeted = [after, before, twin] + [along(k) for k in range(1, spaces)]
+    for device in greeted:
+        pl.semaphore_signal(barrier, inc=1, device_id=device, device_id_type=pl.DeviceIdType.MESH)
+    pl.semaphore_wait(barrier, len(greeted))
+
+    def swap_feats(sent):
+        peer = {"space": spaces - 1 if sent == 1 else 0}
+        return remote(feats.at[:, sent], xbuf.at[:, 1 - sent], feat_send, feat_recv, peer)
+
+    def swap_labels(sent):
+        peer = {"space": spaces - 1 if sent == 1 else 0}
+        return remote(labels.at[sent], lab.at[1 - sent], lab_send, lab_recv, peer)
+
+    for place, sent in ((0, 1), (spaces - 1, 0)):
+        @pl.when(space == place)
+        def _(sent=sent):
+            @pl.when(section == 0)
+            def _():
+                swap_feats(sent).start()
+                xbuf[:, 1 - sent] = feats[:, 1 - sent]
+            swap_labels(sent).start()
+            lab[1 - sent] = labels[1 - sent]
+
+    is_end = (space == 0) | (space == spaces - 1)
+
+    @pl.when(jnp.logical_not(is_end))
+    def _():
+        @pl.when(section == 0)
+        def _():
+            xbuf[...] = feats[...]
+        lab[...] = labels[...]
+
+    @pl.when(section == last)
+    def _():
+        gbuf[...] = jnp.zeros_like(gbuf)
+
+    total[pl.ds(EXTRA, 128)] = jnp.zeros((128, total.shape[1]), F32)
+
+    for place, sent in ((0, 1), (spaces - 1, 0)):
+        @pl.when(space == place)
+        def _(sent=sent):
+            @pl.when(section == 0)
+            def _():
+                swap_feats(sent).wait()
+            swap_labels(sent).wait()
+
+    coupled = jnp.where(is_end, 1.0, 0.0).astype(F32)
+    tap_rows = taps[...].astype(F32)
+
+    def tap(branch, row_tap, col_tap):
+        place = 9 * branch + 3 * (row_tap + 1) + col_tap + 1
+        return tap_rows[place : place + 1]
+
+    def end_tap(row_tap, col_tap):
+        return tap(0, row_tap, col_tap) * coupled
+
+    def x_copy(group):
+        return remote(xout.at[group], xbuf.at[group], x_send.at[group], x_recv.at[group], after)
+
+    def g_copy(group):
+        return remote(gout.at[group], gbuf.at[group], g_send.at[group], g_recv.at[group], before)
+
+    for group in range(GROUPS):
+        @pl.when(section > 0)
+        def _(group=group):
+            x_copy(group).wait_recv()
+
+        flat = xbuf[group].reshape(pixels, -1)
+        wide_in = flat.astype(F32)
+        halves = (wide_in[:slot_rows], wide_in[slot_rows:])
+        parts = []
+        for branch, spacing in enumerate(spacings):
+            done = []
+            for slot in range(2):
+                running = None
+                for col_tap in (-1, 0, 1):
+                    term = tap(branch, 0, col_tap) * halves[slot]
+                    if branch == 0:
+                        term = term + end_tap(1 - 2 * slot, col_tap) * halves[1 - slot]
+                    term = rows_from(term, col_tap * spacing * step)
+                    running = term if running is None else running + term
+                done.append(running.astype(BF16))
+            mixed = jnp.concatenate(done, axis=0)
+            us[group, branch] = mixed
+            parts.append(jnp.maximum(dot(mixed, point[branch]), 0.0).astype(BF16))
+        parts.append(jnp.maximum(dot(flat, point[3]), 0.0).astype(BF16))
+        joined = jnp.concatenate(parts, axis=1)
+        vs[group] = joined
+        mixed_pre = dot(joined, proj[...])
+        ms[group] = mixed_pre
+        result = (wide_in + jnp.maximum(mixed_pre, 0.0)).astype(BF16)
+        xout[group] = result.reshape(2, slot_rows, -1)
+
+        @pl.when(section < last)
+        def _(group=group):
+            x_copy(group).start()
+
+        logits = dot(head[...], result, NT)
+        rows = [logits[i : i + 1] for i in range(3)]
+        label = jnp.concatenate(
+            [lab[slot, group : group + 1, :slot_rows] for slot in range(2)], axis=1
+        )
+        top = jnp.maximum(jnp.maximum(rows[0], rows[1]), rows[2])
+        powers = [jnp.exp(row - top) for row in rows]
+        below = powers[0] + powers[1] + powers[2]
+        hits = [jnp.where(label == i, 1.0, 0.0).astype(F32) for i in range(3)]
+        weight = sum(hits[i] * class_weight[i].astype(F32) for i in range(3)) * factor
+        deltas = [weight * (powers[i] / below - hits[i]) for i in range(3)]
+        delta = jnp.concatenate(deltas + [jnp.zeros((13, pixels), F32)], axis=0).astype(BF16)
+        hs[group] = dot(delta, head[...], TN)
+        total[pl.ds(HEAD_ROW, 16)] += dot(delta, result)
+
+    for group in range(GROUPS):
+        @pl.when(section < last)
+        def _(group=group):
+            g_copy(group).wait_recv()
+
+        channels = xbuf.shape[3]
+        total_grad = hs[group] + gbuf[group].reshape(pixels, channels).astype(F32)
+        gate_mixed = jnp.where(ms[group] > 0, total_grad, 0.0).astype(BF16)
+        gates = []
+        for branch in range(4):
+            columns = pl.ds(branch * channels, channels)
+            back = dot(gate_mixed, proj[columns], NT)
+            gates.append(jnp.where(vs[group, :, columns] > 0, back, 0.0).astype(BF16))
+        grads = [dot(gates[branch], point[branch], NT).astype(BF16).astype(F32) for branch in range(3)]
+        split = [(grad[:slot_rows], grad[slot_rows:]) for grad in grads]
+
+        @pl.when(section > 0)
+        def _(group=group, gates=gates, total_grad=total_grad, split=split):
+            plain = dot(gates[3], point[3], NT)
+            done = []
+            for slot in range(2):
+                running = None
+                for branch, spacing in enumerate(spacings):
+                    for col_tap in (-1, 0, 1):
+                        term = tap(branch, 0, col_tap) * split[branch][slot]
+                        if branch == 0:
+                            term = term + end_tap(2 * slot - 1, col_tap) * split[branch][1 - slot]
+                        term = rows_from(term, -col_tap * spacing * step)
+                        running = term if running is None else running + term
+                done.append(running)
+            input_grad = total_grad + plain + jnp.concatenate(done, axis=0)
+            gout[group] = input_grad.astype(BF16).reshape(2, slot_rows, channels)
+            g_copy(group).start()
+
+        def put(place, value, group=group):
+            if group == 0:
+                total[place] = value
+            else:
+                total[place] += value
+
+        flat = xbuf[group].reshape(pixels, channels)
+        for branch in range(4):
+            columns = pl.ds(branch * channels, channels)
+            put(pl.ds(1024 + branch * channels, channels), dot(vs[group, :, columns], gate_mixed, TN))
+            source = us[group, branch] if branch < 3 else flat
+            put(columns, dot(source, gates[branch], TN))
+        wide_in = flat.astype(F32)
+        halves = (wide_in[:slot_rows], wide_in[slot_rows:])
+        for branch, spacing in enumerate(spacings):
+            for col_tap in (-1, 0, 1):
+                offset = col_tap * spacing * step
+                row = EXTRA + 9 * branch + col_tap + 1
+                centre = lagged_sum(split[branch][0], halves[0], offset)
+                centre = centre + lagged_sum(split[branch][1], halves[1], offset)
+                total[row + 3 : row + 4] += centre
+                if branch == 0:
+                    for slot in range(2):
+                        cross = lagged_sum(split[0][slot], halves[1 - slot], offset) * coupled
+                        place = row + 6 * (1 - slot)
+                        total[place : place + 1] += cross
+
+    def shard(index):
+        return pl.ds(pl.multiple_of(index * SHARD, 16), SHARD)
+
+    quarter = [lax.rem(space + k, spaces) for k in range(spaces)]
+
+    def pair_copy(k):
+        return remote(
+            wide.at[shard((1 - rep) * spaces + quarter[k])], pair_in.at[shard(quarter[k])],
+            p_send.at[k], p_recv.at[k], twin,
+        )
+
+    def ring_copy(k):
+        return remote(
+            half.at[shard(quarter[k])], ring_in.at[k - 1], r_send.at[k - 1], r_recv.at[k - 1], along(k)
+        )
+
+    def gather_copy(k):
+        mine = shard(rep * spaces + space)
+        return remote(full.at[mine], full.at[mine], a_send.at[k - 1], a_recv.at[k - 1], along(k))
+
+    def cross_copy(k):
+        there = shard(rep * spaces + quarter[k])
+        return remote(full.at[there], full.at[there], c_send.at[k], c_recv.at[k], twin)
+
+    order = [2, 1, 3, 0]
+    for k in order:
+        place = shard((1 - rep) * spaces + quarter[k])
+        wide[place] = total[place].astype(BF16)
+        pair_copy(k).start()
+    for k in order:
+        pair_copy(k).wait_recv()
+        mine = total[shard(rep * spaces + quarter[k])] + pair_in[shard(quarter[k])].astype(F32)
+        if k:
+            half[shard(quarter[k])] = mine.astype(BF16)
+            ring_copy(k).start()
+    for k in range(1, spaces):
+        ring_copy(k).wait_recv()
+        mine = mine + ring_in[k - 1].astype(F32)
+    full[shard(rep * spaces + space)] = mine.astype(BF16)
+    for k in order[:3]:
+        gather_copy(k).start()
+    cross_copy(0).start()
+    for k in (1, 3, 2):
+        gather_copy(k).wait_recv()
+        cross_copy(spaces - k).start()
+    for k in range(spaces):
+        cross_copy(k).wait_recv()
+    for branch in range(4):
+        out_point[branch] = full[pl.ds(256 * branch, 256)].astype(F32)
+    out_proj[...] = full[pl.ds(1024, 1024)].astype(F32)
+    out_extra[...] = full[pl.ds(EXTRA, 48)].astype(F32)
+
+    for group in range(GROUPS):
+        @pl.when(section < last)
+        def _(group=group):
+            x_copy(group).wait_send()
+
+        @pl.when(section > 0)
+        def _(group=group):
+            g_copy(group).wait_send()
+    for k in range(spaces):
+        pair_copy(k).wait_send()
+        cross_copy(k).wait_send()
+        if k:
+            ring_copy(k).wait_send()
+            gather_copy(k).wait_send()
+
+
+def joined_rows_program(
+    feats, labels, class_weight, depth_kernel, point_weight, proj_weight, head_weight
+):
+    snaps, tile_rows, width_cols, channels = feats.shape
+    spaces = lax.axis_size("space")
+    sections = lax.axis_size("section")
+    factor = loss_scale / (snaps * lax.axis_size("rep") * tile_rows * spaces * width_cols)
+    step = tile_rows // GROUPS
+    slot_rows = width_cols * step
+    pixels = snaps * slot_rows
+    maps = feats.reshape(snaps, GROUPS, step, width_cols, channels)
+    maps = maps.transpose(1, 0, 3, 2, 4).reshape(GROUPS, snaps, slot_rows, channels)
+    marks = labels.reshape(snaps, GROUPS, step, width_cols).transpose(0, 1, 3, 2)
+    marks = marks.reshape(snaps, GROUPS, slot_rows)
+    marks = jnp.pad(marks, ((0, 0), (0, 8 - GROUPS), (0, 128 - slot_rows)))
+    taps = depth_kernel.reshape(27, channels)
+    head = jnp.pad(head_weight[0].T, ((0, 13), (0, 0)))
+    vmem = pl.BlockSpec(memory_space=pltpu.VMEM)
+    dma = pltpu.SemaphoreType.DMA
+    outs = pl.pallas_call(
+        functools.partial(block_kernel, factor, spaces, sections),
+        out_shape=(
+            jax.ShapeDtypeStruct((4, channels, channels), F32),
+            jax.ShapeDtypeStruct((4 * channels, channels), F32),
+            jax.ShapeDtypeStruct((48, channels), F32),
+        ),
+        in_specs=[vmem, vmem, pl.BlockSpec(memory_space=pltpu.SMEM), vmem, vmem, vmem, vmem],
+        out_specs=(vmem, vmem, vmem),
+        scratch_shapes=[
+            pltpu.VMEM((GROUPS, 2, slot_rows, channels), BF16),
+            pltpu.VMEM((GROUPS, 2, slot_rows, channels), BF16),
+            pltpu.VMEM((GROUPS, 2, slot_rows, channels), BF16),
+            pltpu.VMEM((GROUPS, 2, slot_rows, channels), BF16),
+            pltpu.VMEM((2, 8, 128), jnp.int32),
+            pltpu.VMEM((GROUPS, 3, pixels, channels), BF16),
+            pltpu.VMEM((GROUPS, pixels, 4 * channels), BF16),
+            pltpu.VMEM((GROUPS, pixels, channels), F32),
+            pltpu.VMEM((GROUPS, pixels, channels), F32),
+            pltpu.VMEM((8 * SHARD, channels), F32),
+            pltpu.VMEM((8 * SHARD, channels), BF16),
+            pltpu.VMEM((4 * SHARD, channels), BF16),
+            pltpu.VMEM((4 * SHARD, channels), BF16),
+            pltpu.VMEM((3, SHARD, channels), BF16),
+            pltpu.VMEM((8 * SHARD, channels), BF16),
+            dma, dma, dma, dma,
+            dma((GROUPS,)), dma((GROUPS,)), dma((GROUPS,)), dma((GROUPS,)),
+            dma((spaces,)), dma((spaces,)),
+            dma((spaces - 1,)), dma((spaces - 1,)),
+            dma((spaces - 1,)), dma((spaces - 1,)),
+            dma((spaces,)), dma((spaces,)),
+        ],
+        compiler_params=pltpu.CompilerParams(
+            collective_id=0, has_side_effects=True, vmem_limit_bytes=40 * 2**20
+        ),
+        cost_estimate=pl.CostEstimate(
+            flops=2 * 2**30, bytes_accessed=8 * 2**20, transcendentals=4096
+        ),
+        name="pyramid_blocks",
+    )(maps, marks, class_weight, taps, point_weight[0], proj_weight[0], head)
+    point_grad, proj_grad, extra = outs
+    kernel_grad = extra[:27].reshape(1, 3, 9, channels)
+    head_grad = extra[32:35].T[None]
+    return kernel_grad, point_grad[None], proj_grad[None], head_grad
+
+
+def rows_pair_up(feats):
+    snaps, tile_rows, width_cols, channels = feats.shape
+    spaces = lax.axis_size("space")
+    return (
+        snaps == 2
+        and (spaces, lax.axis_size("section"), lax.axis_size("rep")) == (4, 4, 2)
+        and spacings[0] == tile_rows * (spaces - 1)
+        and spacings[1] >= tile_rows * spaces
+        and (tile_rows, width_cols, channels) == (4, 40, 256)
+    )
+
+
+def per_device(feats, *others):
+    if rows_pair_up(feats):
+        return joined_rows_program(feats, *others)
+    return general_program(feats, *others)
+
+
 def solution(mesh):
     placed = (
         P("rep", "space", None, None),

time: 264 us -> 73.9 us (0.28)
  starting transfers between devices: 84.4 us -> 0 us
  waiting for transfers between devices: 69.5 us -> 0 us
  Pallas kernels: 0 us -> 63.6 us
  blocking collectives: 27.1 us -> 0 us
  matrix products: 25.3 us -> 0 us
  local copies, waits for them, and re-layouts: 26.4 us -> 8.14 us
  between operations: 16.6 us -> 0.7 us
  other arithmetic: 13.7 us -> 0 us
    ppermute x28 -> x0, starting transfers between devices: 84.4 us -> none  [passed_along(): return lax.ppermute(block, axis, route)]
    pallas_call x0 -> x1, Pallas kernels: none -> 63.6 us  [joined_rows_program(): pl.pallas_call(functools.partial(block_kernel, factor, spaces, sections),...]
    ppermute x28 -> x0, waiting for transfers between devices: 50.6 us -> none  [passed_along(): return lax.ppermute(block, axis, route)]
    psum x1 -> x0, blocking collectives: 27.1 us -> none  [per_device(): lax.psum((local_grads[0], local_grads[1], local_grads[2], local_grads[3])...]
    dot_general x89 -> x0, matrix products: 25.3 us -> none  [the longest x30 12.6 us: outer(): lax.dot_general(first_op, second_op, (((0,), (0,)), ((), ())), preferred_...]
    psum x1 -> x0, waiting for transfers between devices: 18.9 us -> none  [per_device(): lax.psum((local_grads[0], local_grads[1], local_grads[2], local_grads[3])...]
    unnamed x251 -> x16, local copies, waits for them, and re-layouts: 21 us -> 6.09 us
    reduce_sum x16 -> x0, other arithmetic: 4.88 us -> none  [the longest x10 4.65 us: backward_taps(): kernel_rows.append(jnp.sum(partial_sum, axis=0))]
  transfers between devices with their start and end apart: 29 -> 0, of which waited for: 18 -> 0; matrix products, arithmetic and copies ran while one was open for 9% -> 0% of each run, Pallas kernels for 0% -> 0%
where the time goes in v1:
time: 73.9 us; the launch traced here: 72.5 us
  Pallas kernels  63.6 us (86%)
  local copies, waits for them, and re-layouts  8.14 us (11%)
    pallas_call x1, Pallas kernels, joined_rows_program(): pl.pallas_call(functools.partial(block_kernel, factor, spaces, sections),...  63.6 us
    unnamed x16, local copies, waits for them, and re-layouts  6.09 us

profile of v1, /device:TPU:0, one launch (start us, length us, event | category | flops | bytes accessed | tf_op | source)
XLA Modules:
  0.0 72.5 jit_solution(267142415265433643)
XLA Ops:
  0.6 0.0 copy-start
  0.6 1.1 %copy.22 = bf16[2,2,2,40,256]{4,2,3,0,1:T(2,128)(2,1)S(1)} copy(bf16[2,2,2,40,256]{4,3,2,1,0:T(8,128)(2,1)} %bitcast.25) | data formatting | bytes 327680 | tf_op jit(solution)/shard_map/reshape | solution.py:554
  1.7 0.0 copy-start.4
  1.8 0.1 reshape.27.feats
  1.8 0.6 copy-done.4
  2.4 0.1 copy.17
  2.5 0.0 copy-start.3
  2.6 0.1 reshape.29
  2.7 0.6 copy-done.3
  3.3 0.0 copy-start.5
  3.3 0.7 copy-done.5
  4.0 0.0 copy-start.2
  4.0 0.0 copy-done
  4.0 0.6 copy-done.2
  4.6 0.0 copy-start.1
  4.6 1.0 %copy-done.1 = bf16[1,1024,256]{2,1,0:T(8,128)(2,1)S(1)} copy-done((bf16[1,1024,256]{2,1,0:T(8,128)(2,1)S(1)}, bf16[1,1024,256]{2,1,0:T(8,128)(2,1)}, u32[]{:S(2)}) %copy-start.1) | copy-done | bytes 524312
  5.7 63.6 %pyramid_blocks.1 = (f32[4,256,256]{2,1,0:T(8,128)S(1)}, f32[1024,256]{1,0:T(8,128)S(1)}, f32[48,256]{1,0:T(8,128)S(1)}) custom-call(bf16[2,2,80,256]{3,2,1,0:T(8,128)(2,1)S(1)} %reshape.27.feats, s32[2,8,128]{2,1,0:T(8,128)S(1)} %pad.8.labels, s32[3]{0:T(128)S(1)} %copy-done.2, bf16[27,256]{1,0:T(8,128)(2,1)S(1)} %reshape.30.taps, ...), custom_call_target="tpu_custom_call" | custom-call | flops 2147483648 | bytes 8388608 | tf_op jit(solution)/shard_map/pyramid_blocks/pallas_call | solution.py:563
  69.3 0.6 reshape.32
  69.9 0.6 copy.20
  70.5 1.0 %copy.25 = f32[1,4,256,256]{3,2,1,0:T(8,128)} copy(f32[1,4,256,256]{3,2,1,0:T(8,128)S(1)} %bitcast.20) | data formatting | bytes 2097152
  71.5 1.0 %copy.26 = f32[1,1024,256]{2,1,0:T(8,128)} copy(f32[1,1024,256]{2,1,0:T(8,128)S(1)} %bitcast.19) | data formatting | bytes 2097152
  (6 shorter events, 0.0 us)
Async XLA Ops:
  0.6 3.3 %copy-start = (bf16[1,4,256,256]{3,2,1,0:T(8,128)(2,1)S(1)}, bf16[1,4,256,256]{3,2,1,0:T(8,128)(2,1)}, u32[]{:S(2)}) copy-start(bf16[1,4,256,256]{3,2,1,0:T(8,128)(2,1)} %param.11) | copy-start | bytes 1572868
  1.7 0.7 copy-start.4
  2.5 0.7 %copy-start.3 = (bf16[1,3,9,256]{3,1,2,0:T(4,128)(2,1)S(1)}, bf16[1,3,9,256]{3,1,2,0:T(4,128)(2,1)}, u32[]{:S(2)}) copy-start(bf16[1,3,9,256]{3,1,2,0:T(4,128)(2,1)} %param.10) | copy-start | bytes 41476
  3.3 0.7 copy-start.5
  4.0 0.7 copy-start.2
  4.6 1.0 %copy-start.1 = (bf16[1,1024,256]{2,1,0:T(8,128)(2,1)S(1)}, bf16[1,1024,256]{2,1,0:T(8,128)(2,1)}, u32[]{:S(2)}) copy-start(bf16[1,1024,256]{2,1,0:T(8,128)(2,1)} %param.12) | copy-start | bytes 1572868

commit v2 on v1

--- a/solution.py
+++ b/solution.py
@@ -241,6 +241,7 @@
 
 GROUPS = 2
 SHARD = 272
+PIECES = ((0, 144), (144, 128))
 EXTRA = 2048
 HEAD_ROW = EXTRA + 32
 NT = (((1,), (1,)), ((), ()))
@@ -271,12 +272,28 @@
     return lax.dot_general(first, second, dims, preferred_element_type=F32)
 
 
+def unit_rows(rows, columns):
+    down = lax.broadcasted_iota(jnp.int32, (rows, columns), 0)
+    across = lax.broadcasted_iota(jnp.int32, (rows, columns), 1)
+    return jnp.where(down == across, 1.0, 0.0).astype(BF16)
+
+
+def widen_kernel(summed, kernel_grad, point_grad, proj_grad, head_grad):
+    for branch in range(4):
+        point_grad[branch] = summed[pl.ds(256 * branch, 256)].astype(F32)
+    proj_grad[...] = summed[pl.ds(1024, 1024)].astype(F32)
+    rows = summed[pl.ds(EXTRA, 32)].astype(F32)
+    for branch in range(3):
+        kernel_grad[branch] = rows[9 * branch : 9 * branch + 9]
+    head_grad[...] = dot(summed[pl.ds(HEAD_ROW, 16)], unit_rows(16, 3), TN)
+
+
 def block_kernel(
     factor, spaces, sections,
-    feats, labels, class_weight, taps, point, proj, head,
-    out_point, out_proj, out_extra,
-    xbuf, gbuf, xout, gout, lab, us, vs, ms, hs, total, wide, pair_in, half, ring_in, full,
-    feat_send, feat_recv, lab_send, lab_recv, x_send, x_recv, g_send, g_recv,
+    feats, labels, class_weight, small_in, point_in, proj_in,
+    full,
+    small, point, proj, raw, xbuf, gbuf, xout, gout, lab, us, vs, ms, hs, total, wide, pair_in, half, ring_in,
+    load_sems, feat_send, feat_recv, lab_send, lab_recv, x_send, x_recv, g_send, g_recv,
     p_send, p_recv, r_send, r_recv, a_send, a_recv, c_send, c_recv,
 ):
     space = lax.axis_index("space")
@@ -299,38 +316,56 @@
             device_id=device, device_id_type=pl.DeviceIdType.MESH,
         )
 
+    loads = [
+        pltpu.make_async_copy(source, target, load_sems.at[i])
+        for i, (source, target) in enumerate(
+            ((small_in, small), (point_in, point), (proj_in, proj))
+        )
+    ]
+    for load in loads:
+        load.start()
+
     barrier = pltpu.get_barrier_semaphore()
     greeted = [after, before, twin] + [along(k) for k in range(1, spaces)]
     for device in greeted:
         pl.semaphore_signal(barrier, inc=1, device_id=device, device_id_type=pl.DeviceIdType.MESH)
     pl.semaphore_wait(barrier, len(greeted))
 
-    def swap_feats(sent):
+    def swap_feats(sent, group):
         peer = {"space": spaces - 1 if sent == 1 else 0}
-        return remote(feats.at[:, sent], xbuf.at[:, 1 - sent], feat_send, feat_recv, peer)
+        rows = pl.ds(2 * group, 2)
+        return remote(
+            feats.at[sent, rows], raw.at[1 - sent, rows], feat_send.at[group], feat_recv.at[group], peer
+        )
 
     def swap_labels(sent):
         peer = {"space": spaces - 1 if sent == 1 else 0}
         return remote(labels.at[sent], lab.at[1 - sent], lab_send, lab_recv, peer)
 
-    for place, sent in ((0, 1), (spaces - 1, 0)):
+    def keep(source, target, index, slot):
+        return pltpu.make_async_copy(source.at[slot], target.at[slot], load_sems.at[4 + 2 * index + slot])
+
+    ends = ((0, 1), (spaces - 1, 0))
+    for place, sent in ends:
         @pl.when(space == place)
         def _(sent=sent):
             @pl.when(section == 0)
             def _():
-                swap_feats(sent).start()
-                xbuf[:, 1 - sent] = feats[:, 1 - sent]
+                for group in range(GROUPS):
+                    swap_feats(sent, group).start()
+                keep(feats, raw, 0, 1 - sent).start()
             swap_labels(sent).start()
-            lab[1 - sent] = labels[1 - sent]
+            keep(labels, lab, 1, 1 - sent).start()
 
     is_end = (space == 0) | (space == spaces - 1)
 
     @pl.when(jnp.logical_not(is_end))
     def _():
-        @pl.when(section == 0)
-        def _():
-            xbuf[...] = feats[...]
-        lab[...] = labels[...]
+        for slot in range(2):
+            @pl.when(section == 0)
+            def _(slot=slot):
+                keep(feats, raw, 0, slot).start()
+            keep(labels, lab, 1, slot).start()
 
     @pl.when(section == last)
     def _():
@@ -338,20 +373,43 @@
 
     total[pl.ds(EXTRA, 128)] = jnp.zeros((128, total.shape[1]), F32)
 
-    for place, sent in ((0, 1), (spaces - 1, 0)):
+    for place, sent in ends:
         @pl.when(space == place)
         def _(sent=sent):
             @pl.when(section == 0)
             def _():
-                swap_feats(sent).wait()
+                keep(feats, raw, 0, 1 - sent).wait()
+            keep(labels, lab, 1, 1 - sent).wait()
             swap_labels(sent).wait()
 
+    @pl.when(jnp.logical_not(is_end))
+    def _():
+        for slot in range(2):
+            @pl.when(section == 0)
+            def _(slot=slot):
+                keep(feats, raw, 0, slot).wait()
+            keep(labels, lab, 1, slot).wait()
+
+    for load in loads:
+        load.wait()
+
     coupled = jnp.where(is_end, 1.0, 0.0).astype(F32)
-    tap_rows = taps[...].astype(F32)
+    tap_rows = small[pl.ds(0, 32)].astype(F32)
+    head_rows = small[pl.ds(32, 16)]
 
     def tap(branch, row_tap, col_tap):
         place = 9 * branch + 3 * (row_tap + 1) + col_tap + 1
         return tap_rows[place : place + 1]
+
+    place = lax.broadcasted_iota(jnp.int32, (slot_rows, slot_rows), 0)
+    origin = lax.broadcasted_iota(jnp.int32, (slot_rows, slot_rows), 1)
+    permute = jnp.where(origin == (place & 1) * 40 + (place >> 1), 1.0, 0.0).astype(BF16)
+
+    column = lax.broadcasted_iota(jnp.int32, (40, slot_rows), 0)
+    target = lax.broadcasted_iota(jnp.int32, (40, slot_rows), 1)
+    doubled = jnp.where((target >> 1) == column, 1.0, 0.0).astype(BF16)
+    odd = (lax.broadcasted_iota(jnp.int32, (1, slot_rows), 1) & 1) == 1
+    marks = [dot(lab[slot].astype(F32).astype(BF16), doubled) for slot in range(2)]
 
     def end_tap(row_tap, col_tap):
         return tap(0, row_tap, col_tap) * coupled
@@ -366,6 +424,18 @@
         @pl.when(section > 0)
         def _(group=group):
             x_copy(group).wait_recv()
+
+        for place, sent in ends:
+            @pl.when((section == 0) & (space == place))
+            def _(sent=sent, group=group):
+                swap_feats(sent, group).wait()
+
+        @pl.when(section == 0)
+        def _(group=group):
+            for slot in range(2):
+                rows = raw[slot, 2 * group : 2 * group + 2].astype(F32)
+                rows = rows.reshape(slot_rows, -1).astype(BF16)
+                xbuf[group, slot] = dot(permute, rows).astype(BF16)
 
         flat = xbuf[group].reshape(pixels, -1)
         wide_in = flat.astype(F32)
@@ -397,19 +467,23 @@
         def _(group=group):
             x_copy(group).start()
 
-        logits = dot(head[...], result, NT)
+        logits = dot(head_rows, result, NT)
         rows = [logits[i : i + 1] for i in range(3)]
         label = jnp.concatenate(
-            [lab[slot, group : group + 1, :slot_rows] for slot in range(2)], axis=1
+            [
+                jnp.where(odd, mark[2 * group + 1 : 2 * group + 2], mark[2 * group : 2 * group + 1])
+                for mark in marks
+            ],
+            axis=1,
         )
         top = jnp.maximum(jnp.maximum(rows[0], rows[1]), rows[2])
         powers = [jnp.exp(row - top) for row in rows]
         below = powers[0] + powers[1] + powers[2]
-        hits = [jnp.where(label == i, 1.0, 0.0).astype(F32) for i in range(3)]
+        hits = [jnp.where(label == float(i), 1.0, 0.0).astype(F32) for i in range(3)]
         weight = sum(hits[i] * class_weight[i].astype(F32) for i in range(3)) * factor
         deltas = [weight * (powers[i] / below - hits[i]) for i in range(3)]
         delta = jnp.concatenate(deltas + [jnp.zeros((13, pixels), F32)], axis=0).astype(BF16)
-        hs[group] = dot(delta, head[...], TN)
+        hs[group] = dot(delta, head_rows, TN)
         total[pl.ds(HEAD_ROW, 16)] += dot(delta, result)
 
     for group in range(GROUPS):
@@ -473,57 +547,70 @@
                         place = row + 6 * (1 - slot)
                         total[place : place + 1] += cross
 
-    def shard(index):
-        return pl.ds(pl.multiple_of(index * SHARD, 16), SHARD)
+    def shard(index, piece):
+        start, length = PIECES[piece]
+        return pl.ds(pl.multiple_of(index * SHARD + start, 16), length)
 
     quarter = [lax.rem(space + k, spaces) for k in range(spaces)]
 
-    def pair_copy(k):
+    def pair_copy(k, piece):
         return remote(
-            wide.at[shard((1 - rep) * spaces + quarter[k])], pair_in.at[shard(quarter[k])],
-            p_send.at[k], p_recv.at[k], twin,
-        )
-
-    def ring_copy(k):
+            wide.at[shard((1 - rep) * spaces + quarter[k], piece)],
+            pair_in.at[shard(quarter[k], piece)],
+            p_send.at[piece, k], p_recv.at[piece, k], twin,
+        )
+
+    def ring_copy(k, piece):
         return remote(
-            half.at[shard(quarter[k])], ring_in.at[k - 1], r_send.at[k - 1], r_recv.at[k - 1], along(k)
-        )
-
-    def gather_copy(k):
-        mine = shard(rep * spaces + space)
-        return remote(full.at[mine], full.at[mine], a_send.at[k - 1], a_recv.at[k - 1], along(k))
-
-    def cross_copy(k):
-        there = shard(rep * spaces + quarter[k])
-        return remote(full.at[there], full.at[there], c_send.at[k], c_recv.at[k], twin)
+            half.at[shard(quarter[k], piece)], ring_in.at[k - 1, pl.ds(*PIECES[piece])],
+            r_send.at[piece, k - 1], r_recv.at[piece, k - 1], along(k),
+        )
+
+    def gather_copy(k, piece):
+        mine = shard(rep * spaces + space, piece)
+        return remote(
+            full.at[mine], full.at[mine], a_send.at[piece, k - 1], a_recv.at[piece, k - 1], along(k)
+        )
+
+    def cross_copy(k, piece):
+        there = shard(rep * spaces + quarter[k], piece)
+        return remote(
+            full.at[there], full.at[there], c_send.at[piece, k], c_recv.at[piece, k], twin
+        )
 
     order = [2, 1, 3, 0]
-    for k in order:
-        place = shard((1 - rep) * spaces + quarter[k])
-        wide[place] = total[place].astype(BF16)
-        pair_copy(k).start()
-    for k in order:
-        pair_copy(k).wait_recv()
-        mine = total[shard(rep * spaces + quarter[k])] + pair_in[shard(quarter[k])].astype(F32)
-        if k:
-            half[shard(quarter[k])] = mine.astype(BF16)
-            ring_copy(k).start()
-    for k in range(1, spaces):
-        ring_copy(k).wait_recv()
-        mine = mine + ring_in[k - 1].astype(F32)
-    full[shard(rep * spaces + space)] = mine.astype(BF16)
-    for k in order[:3]:
-        gather_copy(k).start()
-    cross_copy(0).start()
-    for k in (1, 3, 2):
-        gather_copy(k).wait_recv()
-        cross_copy(spaces - k).start()
-    for k in range(spaces):
-        cross_copy(k).wait_recv()
-    for branch in range(4):
-        out_point[branch] = full[pl.ds(256 * branch, 256)].astype(F32)
-    out_proj[...] = full[pl.ds(1024, 1024)].astype(F32)
-    out_extra[...] = full[pl.ds(EXTRA, 48)].astype(F32)
+    both = range(len(PIECES))
+    for piece in both:
+        for k in order:
+            place = shard((1 - rep) * spaces + quarter[k], piece)
+            wide[place] = total[place].astype(BF16)
+            pair_copy(k, piece).start()
+    kept = []
+    for piece in both:
+        for k in order:
+            pair_copy(k, piece).wait_recv()
+            place = shard(quarter[k], piece)
+            mine = total[shard(rep * spaces + quarter[k], piece)] + pair_in[place].astype(F32)
+            if k:
+                half[place] = mine.astype(BF16)
+                ring_copy(k, piece).start()
+        kept.append(mine)
+    for piece in both:
+        mine = kept[piece]
+        for k in range(1, spaces):
+            ring_copy(k, piece).wait_recv()
+            mine = mine + ring_in[k - 1, pl.ds(*PIECES[piece])].astype(F32)
+        full[shard(rep * spaces + space, piece)] = mine.astype(BF16)
+        for k in order[:3]:
+            gather_copy(k, piece).start()
+        cross_copy(0, piece).start()
+    for piece in both:
+        for k in (1, 3, 2):
+            gather_copy(k, piece).wait_recv()
+            cross_copy(spaces - k, piece).start()
+    for piece in both:
+        for k in range(spaces):
+            cross_copy(k, piece).wait_recv()
 
     for group in range(GROUPS):
         @pl.when(section < last)
@@ -533,12 +620,13 @@
         @pl.when(section > 0)
         def _(group=group):
             g_copy(group).wait_send()
-    for k in range(spaces):
-        pair_copy(k).wait_send()
-        cross_copy(k).wait_send()
-        if k:
-            ring_copy(k).wait_send()
-            gather_copy(k).wait_send()
+    for piece in both:
+        for k in range(spaces):
+            pair_copy(k, piece).wait_send()
+            cross_copy(k, piece).wait_send()
+            if k:
+                ring_copy(k, piece).wait_send()
+                gather_copy(k, piece).wait_send()
 
 
 def joined_rows_program(
@@ -551,30 +639,26 @@
     step = tile_rows // GROUPS
     slot_rows = width_cols * step
     pixels = snaps * slot_rows
-    maps = feats.reshape(snaps, GROUPS, step, width_cols, channels)
-    maps = maps.transpose(1, 0, 3, 2, 4).reshape(GROUPS, snaps, slot_rows, channels)
-    marks = labels.reshape(snaps, GROUPS, step, width_cols).transpose(0, 1, 3, 2)
-    marks = marks.reshape(snaps, GROUPS, slot_rows)
-    marks = jnp.pad(marks, ((0, 0), (0, 8 - GROUPS), (0, 128 - slot_rows)))
-    taps = depth_kernel.reshape(27, channels)
-    head = jnp.pad(head_weight[0].T, ((0, 13), (0, 0)))
+    small = jnp.pad(depth_kernel.reshape(27, channels), ((0, 21), (0, 0)))
+    small = small + jnp.pad(head_weight[0].T, ((32, 13), (0, 0)))
     vmem = pl.BlockSpec(memory_space=pltpu.VMEM)
+    far = pl.BlockSpec(memory_space=pl.ANY)
     dma = pltpu.SemaphoreType.DMA
     outs = pl.pallas_call(
         functools.partial(block_kernel, factor, spaces, sections),
-        out_shape=(
-            jax.ShapeDtypeStruct((4, channels, channels), F32),
-            jax.ShapeDtypeStruct((4 * channels, channels), F32),
-            jax.ShapeDtypeStruct((48, channels), F32),
-        ),
-        in_specs=[vmem, vmem, pl.BlockSpec(memory_space=pltpu.SMEM), vmem, vmem, vmem, vmem],
-        out_specs=(vmem, vmem, vmem),
+        out_shape=jax.ShapeDtypeStruct((8 * SHARD, channels), BF16),
+        in_specs=[far, far, pl.BlockSpec(memory_space=pltpu.SMEM), far, far, far],
+        out_specs=vmem,
         scratch_shapes=[
+            pltpu.VMEM((48, channels), BF16),
+            pltpu.VMEM(point_weight.shape[1:], BF16),
+            pltpu.VMEM(proj_weight.shape[1:], BF16),
+            pltpu.VMEM(feats.shape, BF16),
             pltpu.VMEM((GROUPS, 2, slot_rows, channels), BF16),
             pltpu.VMEM((GROUPS, 2, slot_rows, channels), BF16),
             pltpu.VMEM((GROUPS, 2, slot_rows, channels), BF16),
             pltpu.VMEM((GROUPS, 2, slot_rows, channels), BF16),
-            pltpu.VMEM((2, 8, 128), jnp.int32),
+            pltpu.VMEM(labels.shape, jnp.int32),
             pltpu.VMEM((GROUPS, 3, pixels, channels), BF16),
             pltpu.VMEM((GROUPS, pixels, 4 * channels), BF16),
             pltpu.VMEM((GROUPS, pixels, channels), F32),
@@ -584,26 +668,35 @@
             pltpu.VMEM((4 * SHARD, channels), BF16),
             pltpu.VMEM((4 * SHARD, channels), BF16),
             pltpu.VMEM((3, SHARD, channels), BF16),
-            pltpu.VMEM((8 * SHARD, channels), BF16),
-            dma, dma, dma, dma,
+            dma((8,)), dma((GROUPS,)), dma((GROUPS,)), dma, dma,
             dma((GROUPS,)), dma((GROUPS,)), dma((GROUPS,)), dma((GROUPS,)),
-            dma((spaces,)), dma((spaces,)),
-            dma((spaces - 1,)), dma((spaces - 1,)),
-            dma((spaces - 1,)), dma((spaces - 1,)),
-            dma((spaces,)), dma((spaces,)),
+            dma((len(PIECES), spaces)), dma((len(PIECES), spaces)),
+            dma((len(PIECES), spaces - 1)), dma((len(PIECES), spaces - 1)),
+            dma((len(PIECES), spaces - 1)), dma((len(PIECES), spaces - 1)),
+            dma((len(PIECES), spaces)), dma((len(PIECES), spaces)),
         ],
         compiler_params=pltpu.CompilerParams(
-            collective_id=0, has_side_effects=True, vmem_limit_bytes=40 * 2**20
+            collective_id=0, has_side_effects=True, vmem_limit_bytes=62 * 2**20
         ),
         cost_estimate=pl.CostEstimate(
             flops=2 * 2**30, bytes_accessed=8 * 2**20, transcendentals=4096
         ),
         name="pyramid_blocks",
-    )(maps, marks, class_weight, taps, point_weight[0], proj_weight[0], head)
-    point_grad, proj_grad, extra = outs
-    kernel_grad = extra[:27].reshape(1, 3, 9, channels)
-    head_grad = extra[32:35].T[None]
-    return kernel_grad, point_grad[None], proj_grad[None], head_grad
+    )(feats, labels, class_weight, small, point_weight[0], proj_weight[0])
+    kernel_grad, point_grad, proj_grad, head_grad = pl.pallas_call(
+        widen_kernel,
+        out_shape=(
+            jax.ShapeDtypeStruct((3, 9, channels), F32),
+            jax.ShapeDtypeStruct((4, channels, channels), F32),
+            jax.ShapeDtypeStruct((4 * channels, channels), F32),
+            jax.ShapeDtypeStruct((channels, 3), F32),
+        ),
+        in_specs=[vmem],
+        out_specs=(vmem, vmem, vmem, vmem),
+        compiler_params=pltpu.CompilerParams(vmem_limit_bytes=16 * 2**20),
+        name="widen",
+    )(outs)
+    return kernel_grad[None], point_grad[None], proj_grad[None], head_grad[None]
 
 
 def rows_pair_up(feats):

time: 73.9 us -> 72 us (0.974); the launches traced: 72.5 us -> 71.7 us
  local copies, waits for them, and re-layouts: 8.14 us -> 3.28 us
  Pallas kernels: 63.6 us -> 66.5 us
  other arithmetic: 0 us -> 1.3 us
    unnamed x16 -> x5, local copies, waits for them, and re-layouts: 6.09 us -> 3.26 us
    reshape x6 -> x1, local copies, waits for them, and re-layouts: 2.04 us -> 0.01 us  [joined_rows_program(): small = jnp.pad(depth_kernel.reshape(27, channels), ((0, 21), (0, 0)))]
    pallas_call x0 -> x1, Pallas kernels: none -> 1.43 us  [joined_rows_program(): pl.pallas_call(widen_kernel, out_shape=(jax.ShapeDtypeStruct((3, 9, chann...]
    pallas_call x1, Pallas kernels: 63.6 us -> 65 us  [joined_rows_program(): pl.pallas_call(functools.partial(block_kernel, factor, spaces, sections),...]
    add x0 -> x1, other arithmetic: none -> 1.3 us  [joined_rows_program(): small = small + jnp.pad(head_weight[0].T, ((32, 13), (0, 0)))]
where the time goes in v2:
time: 72 us; the launch traced here: 71.7 us
  Pallas kernels  66.5 us (92%)
  local copies, waits for them, and re-layouts  3.28 us (5%)
  other arithmetic  1.3 us (2%)
    pallas_call x1, Pallas kernels, joined_rows_program(): pl.pallas_call(functools.partial(block_kernel, factor, spaces, sections),...  65 us
    unnamed x5, local copies, waits for them, and re-layouts  3.26 us

profile of v2, /device:TPU:0, one launch (start us, length us, event | category | flops | bytes accessed | tf_op | source)
XLA Modules:
  0.0 71.7 jit_solution(18202216403147136184)
XLA Ops:
  0.6 0.7 %copy.14 = bf16[1,3,9,256]{3,2,1,0:T(8,128)(2,1)S(1)} copy(bf16[1,3,9,256]{3,1,2,0:T(4,128)(2,1)} %param.10) | data formatting | bytes 27648 | tf_op args[3]
  1.4 1.3 %pad_add_fusion.small_in = bf16[48,256]{1,0:T(8,128)(2,1)} fusion(bf16[3,256]{1,0:T(4,128)(2,1)} %bitcast.11, bf16[27,256]{1,0:T(8,128)(2,1)S(1)} %reshape.11), kind=kLoop, calls=%fused_computation | loop fusion | flops 49152 | bytes 39936 | tf_op jit(solution)/shard_map/add | solution.py:643
  2.7 65.0 %pyramid_blocks.1.summed = bf16[2176,256]{1,0:T(8,128)(2,1)} custom-call(bf16[2,4,40,256]{3,2,1,0:T(8,128)(2,1)} %feats.1, s32[2,4,40]{2,1,0:T(4,128)} %labels.1, s32[3]{0:T(128)} %class_weight.1, bf16[48,256]{1,0:T(8,128)(2,1)} %pad_add_fusion.small_in, bf16[4,256,256]{2,1,0:T(8,128)(2,1)} %bitcast.14, bf16[1024,256]{1,0:T(8,128)(2,1)} %bitcast.15), custom_call_target="tpu_custom_call" | custom-call | flops 2147483648 | bytes 8388608 | tf_op jit(solution)/shard_map/pyramid_blocks/pallas_call | solution.py:647
  67.7 0.0 copy-start
  67.7 1.2 %copy-done = bf16[2176,256]{1,0:T(8,128)(2,1)S(1)} copy-done((bf16[2176,256]{1,0:T(8,128)(2,1)S(1)}, bf16[2176,256]{1,0:T(8,128)(2,1)}, u32[]{:S(2)}) %copy-start) | copy-done | bytes 1114136
  69.0 1.4 %widen.1 = (f32[3,9,256]{2,1,0:T(8,128)S(1)}, f32[4,256,256]{2,1,0:T(8,128)}, f32[1024,256]{1,0:T(8,128)}, f32[256,3]{1,0:T(8,128)S(1)}) custom-call(bf16[2176,256]{1,0:T(8,128)(2,1)S(1)} %copy-done), custom_call_target="tpu_custom_call" | custom-call | tf_op jit(solution)/shard_map/widen/pallas_call | solution.py:686
  70.4 0.6 copy.15
  71.0 0.7 copy.16
  (1 shorter events, 0.0 us)
Async XLA Ops:
  67.7 1.2 %copy-start = (bf16[2176,256]{1,0:T(8,128)(2,1)S(1)}, bf16[2176,256]{1,0:T(8,128)(2,1)}, u32[]{:S(2)}) copy-start(bf16[2176,256]{1,0:T(8,128)(2,1)} %pyramid_blocks.1.summed) | copy-start | bytes 3342340
